TPU v7x, 32 devices: a whole 2x2x4 slice. The times are simulated.
32 devices in a mesh: expert: 4 (over y, x), dp: 8 (over z, core).
Axes of the slice: x: 2, y: 2, z: 4, core: 2. Of those that a mesh axis runs over, the one named last changes fastest.
Arguments:
- tokens: bfloat16 [512, 4096], P(('expert', 'dp')), may hold values from -6 to 6
- grad_out: bfloat16 [512, 4096], P(('expert', 'dp')), may hold values from -6 to 6
- gate_values: bfloat16 [512, 2], P(('expert', 'dp')), may hold values from 0.099609375 to 1
- routes: int32 [512, 2], P(('expert', 'dp')), may hold values from 0 to 7, all different within a row; in each aligned block of 16 rows (0 to 15, 16 to 31, ...) at most 8 rows name the same one
- gate_weight: bfloat16 [8, 1536, 4096], P('expert', 'dp'), may hold values from -0.09375 to 0.09375
- up_weight: bfloat16 [8, 1536, 4096], P('expert', 'dp'), may hold values from -0.09375 to 0.09375
- down_weight: bfloat16 [8, 1536, 4096], P('expert', 'dp'), may hold values from -0.15625 to 0.15625
Outputs:
- grad_tokens: bfloat16 [512, 4096], P(('expert', 'dp'))
- grad_gates: float32 [512, 2], P(('expert', 'dp'))
- grad_gate_weight: bfloat16 [8, 1536, 4096], P('expert', 'dp')
- grad_up_weight: bfloat16 [8, 1536, 4096], P('expert', 'dp')
- grad_down_weight: bfloat16 [8, 1536, 4096], P('expert', 'dp')
Inputs may be any that keep to these rules, and one draw needn't show every extreme that they name: `routes`: each row names 2 different experts. In each aligned block of 16 rows (the rows of one device) no expert is named by more than 8 rows, a bound that some block reaches.
All inputs are finite; a program needn't handle non-finite values.
Results may differ from a plain program's by a relative error of at most 0.019.
Values may be sent and summed in bfloat16 or wider, within the bound.
A program may use at most 128 MiB of HBM per device.

v0:
```python
import jax
import jax.numpy as jnp
from jax import lax
from jax.sharding import PartitionSpec as P


def per_device(tokens, grad_out, gate_values, routes, gate_weight, up_weight, down_weight):
    tok_rows, model_width = tokens.shape
    chosen = routes.shape[1]
    local_experts = gate_weight.shape[0]
    groups = lax.axis_size("expert")
    replicas = lax.axis_size("dp")
    experts_all = local_experts * groups
    capacity = 2 * tok_rows * chosen // experts_all
    slot_count = experts_all * capacity
    flat_routes = routes.reshape(-1)
    onehot = (flat_routes[:, None] == jnp.arange(experts_all, dtype=jnp.int32)[None, :]).astype(
        jnp.int32
    )
    earlier = jnp.cumsum(onehot, axis=0) - onehot
    slot_rank = jnp.sum(earlier * onehot, axis=1)
    owner_col = flat_routes // local_experts
    local_id = flat_routes % local_experts
    slot_index = (local_id * groups + owner_col) * capacity + slot_rank
    placing = (jnp.arange(slot_count, dtype=jnp.int32)[:, None] == slot_index[None, :]).astype(
        jnp.float32
    )
    token_map = jnp.sum(placing.reshape(slot_count, tok_rows, chosen), axis=2).astype(jnp.bfloat16)
    slot_gates = jnp.dot(
        placing.astype(jnp.bfloat16), gate_values.reshape(-1), preferred_element_type=jnp.float32
    ).astype(jnp.bfloat16)
    x_slots = jnp.dot(token_map, tokens, preferred_element_type=jnp.float32).astype(jnp.bfloat16)
    dy_slots = jnp.dot(token_map, grad_out, preferred_element_type=jnp.float32).astype(jnp.bfloat16)
    block_shape = (local_experts, groups, capacity, model_width)
    arrived = (
        lax.all_to_all(
            x_slots.reshape(block_shape), "expert", split_axis=1, concat_axis=1, tiled=True
        ),
        lax.all_to_all(
            dy_slots.reshape(block_shape), "expert", split_axis=1, concat_axis=1, tiled=True
        ),
        lax.all_to_all(
            slot_gates.reshape(block_shape[:3]), "expert", split_axis=1, concat_axis=1, tiled=True
        ),
    )
    x_rows, dy_rows, gate_rows = (
        lax.all_gather(arrived[0], "dp", axis=2, tiled=True),
        lax.all_gather(arrived[1], "dp", axis=2, tiled=True),
        lax.all_gather(arrived[2], "dp", axis=2, tiled=True),
    )
    row_total = groups * replicas * capacity
    inputs = x_rows.reshape(local_experts, row_total, model_width)
    upstream = dy_rows.reshape(local_experts, row_total, model_width)
    weighting = gate_rows.reshape(local_experts, row_total).astype(jnp.float32)[..., None]
    gate_pre = jnp.einsum("lrd,lhd->lrh", inputs, gate_weight, preferred_element_type=jnp.float32)
    up_pre = jnp.einsum("lrd,lhd->lrh", inputs, up_weight, preferred_element_type=jnp.float32)
    back_hidden = jnp.einsum(
        "lrd,lhd->lrh", upstream, down_weight, preferred_element_type=jnp.float32
    )
    sigmoid_gate = jax.nn.sigmoid(gate_pre)
    activated = gate_pre * sigmoid_gate
    hidden = activated * up_pre
    gate_part = jnp.sum(back_hidden * hidden, axis=2)
    scaled = weighting * back_hidden
    grad_gate_pre = (
        scaled * up_pre * sigmoid_gate * (1.0 + gate_pre * (1.0 - sigmoid_gate))
    ).astype(jnp.bfloat16)
    grad_up_pre = (scaled * activated).astype(jnp.bfloat16)
    weighted_hidden = (weighting * hidden).astype(jnp.bfloat16)
    input_part = jnp.einsum(
        "lrh,lhd->lrd", grad_gate_pre, gate_weight, preferred_element_type=jnp.float32
    )
    input_part = input_part + jnp.einsum(
        "lrh,lhd->lrd", grad_up_pre, up_weight, preferred_element_type=jnp.float32
    )
    grad_gate_weight = jnp.einsum(
        "lrh,lrd->lhd", grad_gate_pre, inputs, preferred_element_type=jnp.float32
    ).astype(jnp.bfloat16)
    grad_up_weight = jnp.einsum(
        "lrh,lrd->lhd", grad_up_pre, inputs, preferred_element_type=jnp.float32
    ).astype(jnp.bfloat16)
    grad_down_weight = jnp.einsum(
        "lrh,lrd->lhd", weighted_hidden, upstream, preferred_element_type=jnp.float32
    ).astype(jnp.bfloat16)
    part_shape = (local_experts, groups, replicas * capacity, model_width)
    summed = lax.psum_scatter(
        input_part.reshape(part_shape).astype(jnp.bfloat16), "dp", scatter_dimension=2, tiled=True
    )
    returned = lax.all_to_all(summed, "expert", split_axis=1, concat_axis=1, tiled=True)
    returned = returned.reshape(slot_count, model_width)
    grad_tokens = lax.dot_general(
        token_map, returned, (((0,), (0,)), ((), ())), preferred_element_type=jnp.float32
    ).astype(jnp.bfloat16)
    gate_share = gate_part.reshape(local_experts, groups, replicas * capacity)
    gate_total = lax.psum(gate_share, "dp")
    own_gates = lax.dynamic_slice_in_dim(gate_total, lax.axis_index("dp") * capacity, capacity, 2)
    gate_back = lax.all_to_all(
        own_gates, "expert", split_axis=1, concat_axis=1, tiled=True
    ).reshape(slot_count)
    grad_gates = jnp.dot(gate_back, placing, precision=lax.Precision.HIGHEST).reshape(
        tok_rows, chosen
    )
    return (grad_tokens, grad_gates, grad_gate_weight, grad_up_weight, grad_down_weight)


def solution(mesh):
    return jax.shard_map(
        per_device,
        mesh=mesh,
        in_specs=(
            P(("expert", "dp"), None),
            P(("expert", "dp"), None),
            P(("expert", "dp"), None),
            P(("expert", "dp"), None),
            P("expert", "dp", None),
            P("expert", "dp", None),
            P("expert", "dp", None),
        ),
        out_specs=(
            P(("expert", "dp"), None),
            P(("expert", "dp"), None),
            P("expert", "dp", None),
            P("expert", "dp", None),
            P("expert", "dp", None),
        ),
        check_vma=False,
    )
```

profile of v0, /device:TPU:0, one launch (start us, length us, event | category | flops | bytes accessed | tf_op | source)
XLA Modules:
  0.0 213.4 jit_solution(12421247876475143042)
XLA Ops:
  7.2 0.0 copy-start
  7.2 0.0 all-gather.5.cloned.1.call-start
  7.2 0.9 copy.73
  8.1 0.1 eq.53
  8.2 0.1 fusion.5
  8.3 0.1 reduce_window_sum.11
  8.4 0.2 select_reduce_fusion
  8.5 0.1 reduce_sum.30
  8.7 0.1 copy.78
  8.8 0.1 convert_reduce_fusion
  8.8 1.2 convolution_convert_fusion.3
  10.1 13.6 %all_to_all.25 = bf16[2,4,8,4096]{3,2,0,1:T(8,128)(2,1)} all-to-all(bf16[2,4,8,4096]{3,2,0,1:T(8,128)(2,1)S(1)} %copy.85), channel_id=1, replica_groups=mesh['expert'=4,'dp'=8] {'expert'}, dimensions={1} | all-to-all | bytes 1048576 | tf_op jit(solution)/shard_map/all_to_all | solution.py:36
  23.7 0.0 all-gather.5.cloned.1.call-update
  23.7 0.0 all-gather.3.cloned.1.call-start
  23.8 1.2 convolution_convert_fusion.4
  25.0 10.4 %all_to_all.26 = bf16[2,4,8,4096]{3,2,0,1:T(8,128)(2,1)} all-to-all(bf16[2,4,8,4096]{3,2,0,1:T(8,128)(2,1)S(1)} %copy.83), channel_id=1, replica_groups=mesh['expert'=4,'dp'=8] {'expert'}, dimensions={1} | all-to-all | bytes 1048576 | tf_op jit(solution)/shard_map/all_to_all | solution.py:39
  35.4 0.0 all-gather.3.cloned.1.call-update
  35.4 0.0 reduce-scatter.4.cloned.1.call-start
  35.5 0.1 copy.79
  35.6 0.1 reshape.149
  35.7 0.1 fusion
  35.8 0.1 reshape.140
  35.9 7.0 %all_to_all.27 = bf16[2,4,8]{2,0,1:T(2,128)(2,1)S(1)} all-to-all(bf16[2,4,8]{2,0,1:T(2,128)(2,1)S(1)} %copy.80), channel_id=1, replica_groups=mesh['expert'=4,'dp'=8] {'expert'}, dimensions={1} | all-to-all | bytes 256 | tf_op jit(solution)/shard_map/all_to_all | solution.py:42
  42.9 0.1 copy.81
  43.0 14.4 %all_gather.9 = bf16[2,4,64]{1,0,2:T(2,128)(2,1)S(1)} all-gather(bf16[2,4,8]{1,0,2:T(2,128)(2,1)S(1)} %copy.81), channel_id=1, replica_groups=mesh['expert'=4,'dp'=8] {'dp'}, dimensions={2}, use_global_device_ids=true | all-gather | bytes 1152 | tf_op jit(solution)/shard_map/all_gather | solution.py:49
  57.4 0.1 copy.82
  57.5 0.1 reshape.148
  57.6 13.4 %all-gather.5.cloned.1.call-done = bf16[2,4,64,4096]{3,2,0,1:T(8,128)(2,1)} async-done(((bf16[2,4,8,4096]{3,2,0,1:T(8,128)(2,1)}), bf16[2,4,64,4096]{3,2,0,1:T(8,128)(2,1)}) %all-gather.5.cloned.1.call-update) | async-done | bytes 4194320 | tf_op jit(solution)/shard_map/all_gather | solution.py:47
  70.9 2.6 %copy.86 = bf16[2,4,64,4096]{3,2,1,0:T(8,128)(2,1)S(1)} copy(bf16[2,4,64,4096]{3,2,0,1:T(8,128)(2,1)} %all-gather.5.cloned.1.call-done) | data formatting | bytes 8388608 | tf_op jit(solution)/shard_map/all_gather | solution.py:47
  73.6 0.0 copy-start.1
  73.6 0.5 copy-done.4
  74.1 1.5 fusion.22
  75.6 0.0 copy-done.1
  75.6 2.3 %fusion.23 = f32[2,256,192]{1,2,0:T(8,128)} fusion(bf16[2,256,4096]{2,1,0:T(8,128)(2,1)S(1)} %bitcast.41, bf16[2,192,4096]{2,1,0:T(8,128)(2,1)S(1)} %copy-done), kind=kOutput, calls=%fused_computation.56 | convolution fusion | flops 805306368 | bytes 7733248 | tf_op jit(solution)/shard_map/lrd,lhd->lrh/dot_general | solution.py:55
  77.9 40.6 %all-gather.3.cloned.1.call-done = bf16[2,4,64,4096]{3,2,0,1:T(8,128)(2,1)} async-done(((bf16[2,4,8,4096]{3,2,0,1:T(8,128)(2,1)}), bf16[2,4,64,4096]{3,2,0,1:T(8,128)(2,1)}) %all-gather.3.cloned.1.call-update) | async-done | bytes 4194320 | tf_op jit(solution)/shard_map/all_gather | solution.py:48
  118.5 2.6 %copy.84 = bf16[2,4,64,4096]{3,2,1,0:T(8,128)(2,1)S(1)} copy(bf16[2,4,64,4096]{3,2,0,1:T(8,128)(2,1)} %all-gather.3.cloned.1.call-done) | data formatting | bytes 8388608 | tf_op jit(solution)/shard_map/all_gather | solution.py:48
  121.1 0.6 copy-done.12
  121.8 2.2 %multiply_reduce_fusion = (f32[2,256]{1,0:T(2,128)}, bf16[2,256,192]{1,2,0:T(8,128)(2,1)S(1)}, bf16[2,256,192]{1,2,0:T(8,128)(2,1)S(1)}) fusion(f32[2,256,192]{1,2,0:T(8,128)S(1)} %fusion.22, f32[2,256,192]{1,2,0:T(8,128)S(1)} %copy-done.6, f32[2,256]{1,0:T(2,128)S(1)} %reshape.148, bf16[2,256,4096]{2,1,0:T(8,128)(2,1)S(1)} %bitcast.44, ...), kind=kOutput, calls=%fused_computation.11 | convolution fusion | flops 806977024 | bytes 8523776 | tf_op jit(solution)/shard_map/lrd,lhd->lrh/dot_general | solution.py:57
  124.0 1.3 fusion.24
  125.4 0.7 copy-done.5
  126.1 1.4 add_convert_fusion
  127.5 5.2 %copy.99 = bf16[2,4,64,4096]{3,1,0,2:T(4,128)(2,1)} copy(bf16[2,4,64,4096]{3,2,1,0:T(8,128)(2,1)S(1)} %bitcast.47) | data formatting | bytes 8388608
  132.6 7.8 %reshape.155 = bf16[64,32768]{1,0:T(8,128)(2,1)} reshape(bf16[64,2,4,4096]{3,2,1,0:T(4,128)(2,1)} %bitcast.46) | data formatting | bytes 8388608
  140.5 0.0 reduce-scatter.4.cloned.1.call-update
  140.5 0.1 iota_compare_fusion.1
  140.6 0.6 eq.65
  141.2 0.8 reshape.146
  141.9 15.0 %psum.7 = f32[2,4,64]{2,1,0:T(4,128)S(1)} all-reduce(f32[2,4,64]{2,1,0:T(4,128)S(1)} %reshape.146), channel_id=1, replica_groups=mesh['expert'=4,'dp'=8] {'dp'}, use_global_device_ids=true, to_apply=%region_5.6 | all-reduce | flops 512 | bytes 4096 | tf_op jit(solution)/shard_map/psum | solution.py:95
  156.9 0.1 constant_dynamic-slice_fusion
  157.0 0.6 copy.89
  157.6 3.6 %all-to-all-start.4 = ((f32[2,4,8]{2,0,1:T(2,128)}), f32[2,4,8]{2,0,1:T(2,128)S(1)}, u32[]{:S(2)}, u32[]{:S(2)}) async-start(f32[2,4,8]{2,0,1:T(2,128)} %copy.89), calls=%async_computation.4 | async-start | bytes 8192 | tf_op jit(solution)/shard_map/all_to_all | solution.py:97
  161.2 5.1 %convolution_convert_fusion.1 = bf16[2,192,4096]{2,1,0:T(8,128)(2,1)} fusion(bf16[2,256,192]{1,2,0:T(8,128)(2,1)} %copy-done.8, bf16[2,256,4096]{2,1,0:T(8,128)(2,1)} %bitcast.42), kind=kOutput, calls=%fused_computation.2 | convolution fusion | flops 806879232 | bytes 7536640 | tf_op jit(solution)/shard_map/lrh,lrd->lhd/dot_general | solution.py:79
  166.4 2.7 %convolution_convert_fusion = bf16[2,192,4096]{2,1,0:T(8,128)(2,1)} fusion(bf16[2,256,4096]{2,1,0:T(8,128)(2,1)S(1)} %bitcast.45, f32[2,256]{1,0:T(2,128)S(1)} %reshape.148, f32[2,256,192]{1,2,0:T(8,128)S(1)} %fusion.22, f32[2,256,192]{1,2,0:T(8,128)S(1)} %copy-done.7), kind=kOutput, calls=%fused_computation.1 | convolution fusion | flops 807567360 | bytes 8128512 | tf_op jit(solution)/shard_map/lrh,lrd->lhd/dot_general | solution.py:82
  169.0 20.6 %reduce-scatter.4.cloned.1.call-done = bf16[8,32768]{1,0:T(8,128)(2,1)} async-done(((bf16[64,32768]{1,0:T(8,128)(2,1)}), bf16[8,32768]{1,0:T(8,128)(2,1)}) %reduce-scatter.4.cloned.1.call-update) | async-done | bytes 524304
  189.6 2.2 %reshape.156 = bf16[8,2,4,4096]{3,2,1,0:T(4,128)(2,1)} reshape(bf16[8,32768]{1,0:T(8,128)(2,1)} %reduce-scatter.4.cloned.1.call-done) | data formatting | bytes 1048576
  191.8 2.1 %copy.87 = bf16[2,4,8,4096]{3,2,0,1:T(8,128)(2,1)} copy(bf16[2,4,8,4096]{3,1,0,2:T(4,128)(2,1)} %bitcast.51) | data formatting | bytes 1048576 | tf_op jit(solution)/shard_map/reduce_scatter | solution.py:86
  194.0 0.0 all-to-all-done.4
  194.0 4.3 %all-to-all-start.3 = ((bf16[2,4,8,4096]{3,2,0,1:T(8,128)(2,1)}), bf16[2,4,8,4096]{3,2,0,1:T(8,128)(2,1)}, u32[]{:S(2)}, u32[]{:S(2)}) async-start(bf16[2,4,8,4096]{3,2,0,1:T(8,128)(2,1)} %copy.87), calls=%async_computation.3 | async-start | bytes 1048576 | tf_op jit(solution)/shard_map/all_to_all | solution.py:89
  198.3 5.0 %convolution_convert_fusion.2 = bf16[2,192,4096]{2,1,0:T(8,128)(2,1)} fusion(bf16[2,256,192]{1,2,0:T(8,128)(2,1)} %copy-done.9, bf16[2,256,4096]{2,1,0:T(8,128)(2,1)} %bitcast.43), kind=kOutput, calls=%fused_computation.3 | convolution fusion | flops 806879232 | bytes 7536640 | tf_op jit(solution)/shard_map/lrh,lrd->lhd/dot_general | solution.py:76
  203.2 0.1 reshape.151
  203.3 0.8 fusion.6
  204.1 0.8 all-to-all-done.3
  204.9 1.1 copy.88
  206.0 0.8 convolution_convert_fusion.5
  (26 shorter events, 0.2 us)
Async XLA Ops:
  7.2 68.5 %copy-start = (bf16[2,192,4096]{2,1,0:T(8,128)(2,1)S(1)}, bf16[2,192,4096]{2,1,0:T(8,128)(2,1)}, u32[]{:S(2)}) copy-start(bf16[2,192,4096]{2,1,0:T(8,128)(2,1)} %param.11) | copy-start | bytes 9437188
  7.2 28.3 %copy-start.11 = (bf16[16,2]{0,1:T(2,128)(2,1)S(1)}, bf16[16,2]{0,1:T(2,128)(2,1)}, u32[]{:S(2)}) copy-start(bf16[16,2]{0,1:T(2,128)(2,1)} %param.9) | copy-start | bytes 196
  7.2 63.7 %all-gather.5.cloned.1.call-start = ((), (), s32[]{:S(2)}) async-start(), calls=%async_computation.7 | async-start | bytes 4718592 | tf_op jit(solution)/shard_map/all_gather | solution.py:47
  23.7 94.8 %all-gather.3.cloned.1.call-start = ((), (), s32[]{:S(2)}) async-start(), calls=%async_computation.6 | async-start | bytes 4718592 | tf_op jit(solution)/shard_map/all_gather | solution.py:48
  35.4 154.2 %reduce-scatter.4.cloned.1.call-start = ((), (), s32[]{:S(2)}) async-start(), calls=%async_computation.8 | async-start | bytes 4718592
  70.9 3.2 %copy-start.4 = (bf16[2,192,4096]{2,1,0:T(8,128)(2,1)S(1)}, bf16[2,192,4096]{2,1,0:T(8,128)(2,1)}, u32[]{:S(2)}) copy-start(bf16[2,192,4096]{2,1,0:T(8,128)(2,1)} %param.12) | copy-start | bytes 9437188
  73.6 2.1 copy-start.1
  118.5 2.6 %copy-start.6 = (f32[2,256,192]{1,2,0:T(8,128)S(1)}, f32[2,256,192]{1,2,0:T(8,128)}, u32[]{:S(2)}) copy-start(f32[2,256,192]{1,2,0:T(8,128)} %fusion.23) | copy-start | bytes 1179652
  118.5 3.3 %copy-start.12 = (bf16[2,192,4096]{2,1,0:T(8,128)(2,1)S(1)}, bf16[2,192,4096]{2,1,0:T(8,128)(2,1)}, u32[]{:S(2)}) copy-start(bf16[2,192,4096]{2,1,0:T(8,128)(2,1)} %param.13) | copy-start | bytes 9437188
  121.1 2.9 %copy-start.2 = (bf16[2,4,64,4096]{3,2,1,0:T(8,128)(2,1)}, bf16[2,4,64,4096]{3,2,1,0:T(8,128)(2,1)S(1)}, u32[]{:S(2)}) copy-start(bf16[2,4,64,4096]{3,2,1,0:T(8,128)(2,1)S(1)} %copy.84) | copy-start | bytes 12582916
  124.0 1.3 copy-start.9
  124.0 1.3 copy-start.8
  124.0 2.0 copy-start.5
  157.6 36.4 %all-to-all-start.4 = ((f32[2,4,8]{2,0,1:T(2,128)}), f32[2,4,8]{2,0,1:T(2,128)S(1)}, u32[]{:S(2)}, u32[]{:S(2)}) async-start(f32[2,4,8]{2,0,1:T(2,128)} %copy.89), calls=%async_computation.4 | async-start | bytes 8192 | tf_op jit(solution)/shard_map/all_to_all | solution.py:97
  161.2 5.1 %copy-start.3 = (bf16[2,4,64,4096]{3,2,1,0:T(8,128)(2,1)S(1)}, bf16[2,4,64,4096]{3,2,1,0:T(8,128)(2,1)}, u32[]{:S(2)}) copy-start(bf16[2,4,64,4096]{3,2,1,0:T(8,128)(2,1)} %copy-done.2) | copy-start | bytes 12582916
  161.2 5.1 %copy-start.7 = (f32[2,256,192]{1,2,0:T(8,128)S(1)}, f32[2,256,192]{1,2,0:T(8,128)}, u32[]{:S(2)}) copy-start(f32[2,256,192]{1,2,0:T(8,128)} %fusion.23) | copy-start | bytes 1179652
  194.0 9.3 %copy-start.10 = (pred[16,2,64]{2,1,0:T(4,128)(4,1)S(1)}, pred[16,2,64]{2,1,0:T(4,128)(4,1)}, u32[]{:S(2)}) copy-start(pred[16,2,64]{2,1,0:T(4,128)(4,1)} %eq.65) | copy-start | bytes 6148
  194.0 10.9 %all-to-all-start.3 = ((bf16[2,4,8,4096]{3,2,0,1:T(8,128)(2,1)}), bf16[2,4,8,4096]{3,2,0,1:T(8,128)(2,1)}, u32[]{:S(2)}, u32[]{:S(2)}) async-start(bf16[2,4,8,4096]{3,2,0,1:T(8,128)(2,1)} %copy.87), calls=%async_computation.3 | async-start | bytes 1048576 | tf_op jit(solution)/shard_map/all_to_all | solution.py:89
Sparse Core Ops, SparseCore 0:
  23.8 47.0 all-gather.4
  72.5 45.9 all-gather.2
  140.6 48.9 reduce-scatter.3
where the time goes:
time: 214 us; the launch traced here: 213 us
  waiting for transfers between devices  75.4 us (35%)
  blocking collectives  60.3 us (28%)
  local copies, waits for them, and re-layouts  29.5 us (14%)
  matrix products  25.7 us (12%)
  between operations  13.9 us (6%)
  starting transfers between devices  8.03 us (4%)
    all_gather x1, waiting for transfers between devices, per_device(): lax.all_gather(arrived[1], 'dp', axis=2, tiled=True)  40.6 us
    unnamed x4, waiting for transfers between devices  20.6 us
    unnamed x31, local copies, waits for them, and re-layouts  18.1 us
    psum x1, blocking collectives, per_device(): gate_total = lax.psum(gate_share, 'dp')  15 us
    all_gather x1, blocking collectives, per_device(): lax.all_gather(arrived[2], 'dp', axis=2, tiled=True)  14.4 us
    all_to_all x1, blocking collectives, per_device(): lax.all_to_all(x_slots.reshape(block_shape), 'expert', split_axis=1, conc...  13.6 us
    all_gather x1, waiting for transfers between devices, per_device(): lax.all_gather(arrived[0], 'dp', axis=2, tiled=True)  13.4 us
    all_to_all x1, blocking collectives, per_device(): lax.all_to_all(dy_slots.reshape(block_shape), 'expert', split_axis=1, con...  10.4 us
  transfers between devices with their start and end apart: 5, of which 4 were waited for; matrix products, arithmetic and copies ran while one was open for 13% of the time, Pallas kernels for 0%

commit v1 on v0

--- a/solution.py
+++ b/solution.py
@@ -4,7 +4,7 @@
 from jax.sharding import PartitionSpec as P
 
 
-def per_device(tokens, grad_out, gate_values, routes, gate_weight, up_weight, down_weight):
+def routed_rows(tokens, grad_out, gate_values, routes, gate_weight, up_weight, down_weight):
     tok_rows, model_width = tokens.shape
     chosen = routes.shape[1]
     local_experts = gate_weight.shape[0]
@@ -14,11 +14,11 @@
     capacity = 2 * tok_rows * chosen // experts_all
     slot_count = experts_all * capacity
     flat_routes = routes.reshape(-1)
-    onehot = (flat_routes[:, None] == jnp.arange(experts_all, dtype=jnp.int32)[None, :]).astype(
-        jnp.int32
-    )
-    earlier = jnp.cumsum(onehot, axis=0) - onehot
-    slot_rank = jnp.sum(earlier * onehot, axis=1)
+    same = flat_routes[:, None] == flat_routes[None, :]
+    pair_index = jnp.arange(flat_routes.shape[0], dtype=jnp.int32)
+    slot_rank = jnp.sum(
+        (same & (pair_index[None, :] < pair_index[:, None])).astype(jnp.int32), axis=1
+    )
     owner_col = flat_routes // local_experts
     local_id = flat_routes % local_experts
     slot_index = (local_id * groups + owner_col) * capacity + slot_rank
@@ -103,6 +103,123 @@
     return (grad_tokens, grad_gates, grad_gate_weight, grad_up_weight, grad_down_weight)
 
 
+def swap(values, masks):
+    total = lax.axis_size("expert") * lax.axis_size("dp")
+    pairs = [(i, i ^ masks[i % 2]) for i in range(total)]
+    return lax.ppermute(values, ("expert", "dp"), pairs)
+
+
+def swap_order():
+    replicas, groups = lax.axis_size("dp"), lax.axis_size("expert")
+    along_dp = []
+    step = replicas // 2
+    while step > 1:
+        along_dp.append((step, step))
+        step //= 2
+    low, high = replicas, replicas * groups // 2
+    across = [(low, high), (high, low)]
+    return along_dp, across
+
+
+def collect(own, axis):
+    along_dp, across = swap_order()
+    block = own
+    for masks in along_dp:
+        block = jnp.concatenate([block, swap(block, masks)], axis=axis)
+    pieces = [block]
+    for masks in across:
+        pieces = pieces + [swap(piece, masks) for piece in pieces]
+    half = jnp.concatenate(pieces, axis=axis)
+    return half, swap(half, (1, 1))
+
+
+def hand_out(half, other, axis):
+    along_dp, across = swap_order()
+
+    def plus(kept, came):
+        return (kept.astype(jnp.float32) + came.astype(jnp.float32)).astype(kept.dtype)
+
+    half = plus(half, swap(other, (1, 1)))
+    for masks in across[::-1] + along_dp[::-1]:
+        kept, sent = jnp.split(half, 2, axis=axis)
+        half = plus(kept, swap(sent, masks))
+    return half
+
+
+def all_tokens(tokens, grad_out, gate_values, routes, gate_weight, up_weight, down_weight):
+    model_width = tokens.shape[1]
+    chosen = routes.shape[1]
+    local_experts, part, _ = gate_weight.shape
+    side = jnp.concatenate(
+        [gate_values.astype(jnp.float32), routes.astype(jnp.float32)], axis=1
+    ).T
+    sides = collect(side, 1)
+    xs = collect(tokens, 0)
+    dys = collect(grad_out, 0)
+    gate_mat = gate_weight.reshape(local_experts * part, model_width)
+    up_mat = up_weight.reshape(local_experts * part, model_width)
+    down_mat = down_weight.reshape(local_experts * part, model_width)
+    over_width = (((1,), (1,)), ((), ()))
+    over_rows = (((0,), (0,)), ((), ()))
+    unit_expert = lax.broadcasted_iota(jnp.int32, (1, local_experts * part), 1) // part
+    input_parts, gate_parts, lefts = [], [], []
+    for x, dy, info in zip(xs, dys, sides):
+        info = info.T
+        gates = info[:, :chosen]
+        named = info[:, chosen:].astype(jnp.int32) - lax.axis_index("expert") * local_experts
+        gate_pre = lax.dot_general(x, gate_mat, over_width, preferred_element_type=jnp.float32)
+        up_pre = lax.dot_general(x, up_mat, over_width, preferred_element_type=jnp.float32)
+        back_hidden = lax.dot_general(
+            dy, down_mat, over_width, preferred_element_type=jnp.float32
+        )
+        weighting = jnp.zeros(gate_pre.shape, jnp.float32)
+        for k in range(chosen):
+            weighting = weighting + jnp.where(
+                named[:, k : k + 1] == unit_expert, gates[:, k : k + 1], 0.0
+            )
+        sigmoid_gate = jax.nn.sigmoid(gate_pre)
+        activated = gate_pre * sigmoid_gate
+        hidden = activated * up_pre
+        product = back_hidden * hidden
+        gate_parts.append(
+            jnp.stack(
+                [
+                    jnp.sum(jnp.where(named[:, k : k + 1] == unit_expert, product, 0.0), axis=1)
+                    for k in range(chosen)
+                ],
+                axis=0,
+            )
+        )
+        scaled = weighting * back_hidden
+        grad_gate_pre = (
+            scaled * up_pre * sigmoid_gate * (1.0 + gate_pre * (1.0 - sigmoid_gate))
+        ).astype(jnp.bfloat16)
+        grad_up_pre = (scaled * activated).astype(jnp.bfloat16)
+        weighted_hidden = (weighting * hidden).astype(jnp.bfloat16)
+        input_part = jnp.dot(grad_gate_pre, gate_mat, preferred_element_type=jnp.float32)
+        input_part = input_part + jnp.dot(grad_up_pre, up_mat, preferred_element_type=jnp.float32)
+        input_parts.append(input_part.astype(jnp.bfloat16))
+        lefts.append((grad_gate_pre, grad_up_pre, weighted_hidden))
+    grad_tokens = hand_out(input_parts[0], input_parts[1], 0)
+    grad_gates = hand_out(gate_parts[0], gate_parts[1], 1).T
+    weight_grads = []
+    for left, right in ((0, xs), (1, xs), (2, dys)):
+        total = sum(
+            lax.dot_general(lefts[i][left], right[i], over_rows, preferred_element_type=jnp.float32)
+            for i in range(2)
+        )
+        weight_grads.append(total.astype(jnp.bfloat16).reshape(gate_weight.shape))
+    return (grad_tokens, grad_gates, *weight_grads)
+
+
+def per_device(tokens, grad_out, gate_values, routes, *weights):
+    tok_rows, chosen = routes.shape
+    capacity = 2 * tok_rows * chosen // (weights[0].shape[0] * lax.axis_size("expert"))
+    slots = weights[0].shape[0] * capacity
+    plan = all_tokens if tok_rows <= slots else routed_rows
+    return plan(tokens, grad_out, gate_values, routes, *weights)
+
+
 def solution(mesh):
     return jax.shard_map(
         per_device,

time: 214 us -> 135 us (0.63)
  blocking collectives: 60.3 us -> 0 us
  starting transfers between devices: 8.03 us -> 36.9 us
  waiting for transfers between devices: 75.4 us -> 52.7 us
  local copies, waits for them, and re-layouts: 29.5 us -> 13.3 us
  between operations: 13.9 us -> 0.92 us
  other arithmetic: 0.51 us -> 5.39 us
    all_gather x2 -> x0, waiting for transfers between devices: 53.9 us -> none  [the longest x1 40.6 us: per_device(): lax.all_gather(arrived[1], 'dp', axis=2, tiled=True)]
    ppermute x0 -> x28, waiting for transfers between devices: none -> 52.7 us  [swap(): return lax.ppermute(values, ('expert', 'dp'), pairs)]
    ppermute x0 -> x28, starting transfers between devices: none -> 36.9 us  [swap(): return lax.ppermute(values, ('expert', 'dp'), pairs)]
    all_to_all x3 -> x0, blocking collectives: 30.9 us -> none  [the longest x1 13.6 us: per_device(): lax.all_to_all(x_slots.reshape(block_shape), 'expert', split_axis=1, conc...]
    unnamed x4 -> x0, waiting for transfers between devices: 20.6 us -> none
    psum x1 -> x0, blocking collectives: 15 us -> none  [per_device(): gate_total = lax.psum(gate_share, 'dp')]
    all_gather x1 -> x0, blocking collectives: 14.4 us -> none  [per_device(): lax.all_gather(arrived[2], 'dp', axis=2, tiled=True)]
    unnamed x31 -> x20, local copies, waits for them, and re-layouts: 18.1 us -> 9.53 us
  transfers between devices with their start and end apart: 5 -> 28, of which waited for: 4 -> 14; matrix products, arithmetic and copies ran while one was open for 13% -> 26% of each run, Pallas kernels for 0% -> 0%
where the time goes in v1:
time: 135 us
  waiting for transfers between devices  52.7 us (39%)
  starting transfers between devices  36.9 us (27%)
  matrix products  25.8 us (19%)
  local copies, waits for them, and re-layouts  13.3 us (10%)
  other arithmetic  5.39 us (4%)
    ppermute x28, waiting for transfers between devices, swap(): return lax.ppermute(values, ('expert', 'dp'), pairs)  52.7 us
    ppermute x28, starting transfers between devices, swap(): return lax.ppermute(values, ('expert', 'dp'), pairs)  36.9 us
    dot_general x6, matrix products, all_tokens(): lax.dot_general(lefts[i][left], right[i], over_rows, preferred_element_ty...  12.2 us
    unnamed x20, local copies, waits for them, and re-layouts  9.53 us
    dot_general x2, matrix products, all_tokens(): lax.dot_general(dy, down_mat, over_width, preferred_element_type=jnp.floa...  3.12 us
    dot_general x2, matrix products, all_tokens(): jnp.dot(grad_up_pre, up_mat, preferred_element_type=jnp.float32)  2.83 us
  transfers between devices with their start and end apart: 28, of which 14 were waited for; matrix products, arithmetic and copies ran while one was open for 26% of the time, Pallas kernels for 0%

profile of v1, /device:TPU:0, one launch (start us, length us, event | category | flops | bytes accessed | tf_op | source)
XLA Modules:
  0.0 135.1 jit_solution(12689895928654232000)
XLA Ops:
  0.6 0.8 convert_element_type.90
  1.5 0.8 convert_element_type.91
  2.3 4.1 %collective-permute-start = (f32[4,16]{1,0:T(4,128)S(1)}, f32[4,16]{1,0:T(4,128)S(1)}, u32[]{:S(2)}, u32[]{:S(2)}) collective-permute-start(f32[4,16]{1,0:T(4,128)S(1)} %maximum_bitcast_fusion), channel_id=1, source_target_pairs={{0,4},{1,5},{2,6},{3,7},{4,0},{5,1},{6,2},{7,3},{8,12},{9,13},{10,... | collective-permute-start | bytes 776 | tf_op jit(solution)/shard_map/ppermute | solution.py:109
  6.5 2.8 %collective-permute-start.5 = (bf16[16,4096]{1,0:T(8,128)(2,1)}, bf16[16,4096]{1,0:T(8,128)(2,1)S(1)}, u32[]{:S(2)}, u32[]{:S(2)}) collective-permute-start(bf16[16,4096]{1,0:T(8,128)(2,1)} %param.8), channel_id=1, source_target_pairs={{0,4},{1,5},{2,6},{3,7},{4,0},{5,1},{6,2},{7,3},{8,12},{9,13},{10,... | collective-permute-start | bytes 393224 | tf_op jit(solution)/shard_map/ppermute | solution.py:109
  9.4 1.6 %collective-permute-start.1 = (f32[4,32]{1,0:T(4,128)S(1)}, f32[4,32]{1,0:T(4,128)S(1)}, u32[]{:S(2)}, u32[]{:S(2)}) collective-permute-start(f32[4,32]{1,0:T(4,128)S(1)} %pad_maximum_fusion.2), channel_id=1, source_target_pairs={{0,2},{1,3},{2,0},{3,1},{4,6},{5,7},{6,4},{7,5},{8,10},{9,11},{10,... | collective-permute-start | bytes 1544 | tf_op jit(solution)/shard_map/ppermute | solution.py:109
  11.0 1.6 %constant_dynamic-update-slice_fusion.11 = (bf16[64,4096]{1,0:T(8,128)(2,1)}, bf16[256,4096]{1,0:T(8,128)(2,1)}) fusion(bf16[16,4096]{1,0:T(8,128)(2,1)} %param.7), kind=kLoop, calls=%fused_computation.69 | loop fusion | bytes 393216
  13.1 1.5 %collective-permute-start.2 = (f32[4,64]{1,0:T(4,128)S(1)}, f32[4,64]{1,0:T(4,128)S(1)}, u32[]{:S(2)}, u32[]{:S(2)}) collective-permute-start(f32[4,64]{1,0:T(4,128)S(1)} %pad_maximum_fusion.3), channel_id=1, source_target_pairs={{0,8},{1,17},{2,10},{3,19},{4,12},{5,21},{6,14},{7,23},{8,0},{9,25... | collective-permute-start | bytes 3080 | tf_op jit(solution)/shard_map/ppermute | solution.py:109
  14.6 1.6 %constant_dynamic-update-slice_fusion.2 = (bf16[64,4096]{1,0:T(8,128)(2,1)}, bf16[256,4096]{1,0:T(8,128)(2,1)}) fusion(bf16[16,4096]{1,0:T(8,128)(2,1)} %param.8), kind=kLoop, calls=%fused_computation.60 | loop fusion | bytes 393216
  16.2 1.5 %collective-permute-start.3 = (f32[4,64]{1,0:T(4,128)S(1)}, f32[4,64]{1,0:T(4,128)S(1)}, u32[]{:S(2)}, u32[]{:S(2)}) collective-permute-start(f32[4,64]{1,0:T(4,128)S(1)} %pad_maximum_fusion.3), channel_id=1, source_target_pairs={{0,16},{1,9},{2,18},{3,11},{4,20},{5,13},{6,22},{7,15},{8,24},{9,1... | collective-permute-start | bytes 3080 | tf_op jit(solution)/shard_map/ppermute | solution.py:109
  18.2 1.5 %collective-permute-done.3 = f32[4,64]{1,0:T(4,128)S(1)} collective-permute-done((f32[4,64]{1,0:T(4,128)S(1)}, f32[4,64]{1,0:T(4,128)S(1)}, u32[]{:S(2)}, u32[]{:S(2)}) %collective-permute-start.3) | collective-permute-done | bytes 1056 | tf_op jit(solution)/shard_map/ppermute | solution.py:109
  19.8 1.5 %collective-permute-done.4 = f32[4,64]{1,0:T(4,128)S(1)} collective-permute-done((f32[4,64]{1,0:T(4,128)S(1)}, f32[4,64]{1,0:T(4,128)S(1)}, u32[]{:S(2)}, u32[]{:S(2)}) %collective-permute-start.4) | collective-permute-done | bytes 1056 | tf_op jit(solution)/shard_map/ppermute | solution.py:109
  21.4 0.9 pad_maximum_fusion.1
  22.3 1.9 %collective-permute-start.11 = (bf16[32,4096]{1,0:T(8,128)(2,1)S(1)}, bf16[32,4096]{1,0:T(8,128)(2,1)S(1)}, u32[]{:S(2)}, u32[]{:S(2)}) collective-permute-start(bf16[32,4096]{1,0:T(8,128)(2,1)S(1)} %pad_maximum_fusion.1), channel_id=1, source_target_pairs={{0,2},{1,3},{2,0},{3,1},{4,6},{5,7},{6,4},{7,5},{8,10},{9,11},{10,... | collective-permute-start | bytes 786440 | tf_op jit(solution)/shard_map/ppermute | solution.py:109
  24.3 0.9 pad_maximum_fusion
  25.4 0.7 constant_dynamic-update-slice_fusion.10
  26.1 0.7 constant_dynamic-update-slice_fusion.1
  26.9 4.6 %collective-permute-done.11 = bf16[32,4096]{1,0:T(8,128)(2,1)S(1)} collective-permute-done((bf16[32,4096]{1,0:T(8,128)(2,1)S(1)}, bf16[32,4096]{1,0:T(8,128)(2,1)S(1)}, u32[]{:S(2)}, u32[]{:S(2)}) %collective-permute-start.11) | collective-permute-done | bytes 262176 | tf_op jit(solution)/shard_map/ppermute | solution.py:109
  31.5 0.8 constant_dynamic-update-slice_fusion.9
  32.9 4.0 %collective-permute-done.6 = bf16[32,4096]{1,0:T(8,128)(2,1)S(1)} collective-permute-done((bf16[32,4096]{1,0:T(8,128)(2,1)S(1)}, bf16[32,4096]{1,0:T(8,128)(2,1)S(1)}, u32[]{:S(2)}, u32[]{:S(2)}) %collective-permute-start.6) | collective-permute-done | bytes 262176 | tf_op jit(solution)/shard_map/ppermute | solution.py:109
  36.8 0.8 constant_dynamic-update-slice_fusion
  38.2 1.4 %collective-permute-start.13 = (bf16[64,4096]{1,0:T(8,128)(2,1)}, bf16[64,4096]{1,0:T(8,128)(2,1)S(1)}, u32[]{:S(2)}, u32[]{:S(2)}) collective-permute-start(bf16[64,4096]{1,0:T(8,128)(2,1)} %get-tuple-element.15), channel_id=1, source_target_pairs={{0,16},{1,9},{2,18},{3,11},{4,20},{5,13},{6,22},{7,15},{8,24},{9,1... | collective-permute-start | bytes 1572872 | tf_op jit(solution)/shard_map/ppermute | solution.py:109
  39.6 0.6 collective-permute-start.8
  40.2 2.6 %collective-permute-done.12 = bf16[64,4096]{1,0:T(8,128)(2,1)S(1)} collective-permute-done((bf16[64,4096]{1,0:T(8,128)(2,1)}, bf16[64,4096]{1,0:T(8,128)(2,1)S(1)}, u32[]{:S(2)}, u32[]{:S(2)}) %collective-permute-start.12) | collective-permute-done | bytes 524320 | tf_op jit(solution)/shard_map/ppermute | solution.py:109
  42.8 0.8 constant_dynamic-update-slice_fusion.14
  43.6 10.4 %collective-permute-done.7 = bf16[64,4096]{1,0:T(8,128)(2,1)S(1)} collective-permute-done((bf16[64,4096]{1,0:T(8,128)(2,1)}, bf16[64,4096]{1,0:T(8,128)(2,1)S(1)}, u32[]{:S(2)}, u32[]{:S(2)}) %collective-permute-start.7) | collective-permute-done | bytes 524320 | tf_op jit(solution)/shard_map/ppermute | solution.py:109
  54.0 0.8 constant_dynamic-update-slice_fusion.5
  54.9 0.8 constant_dynamic-update-slice_fusion.13
  55.7 7.1 %collective-permute-done.14 = bf16[64,4096]{1,0:T(8,128)(2,1)S(1)} collective-permute-done((bf16[64,4096]{1,0:T(8,128)(2,1)S(1)}, bf16[64,4096]{1,0:T(8,128)(2,1)S(1)}, u32[]{:S(2)}, u32[]{:S(2)}) %collective-permute-start.14) | collective-permute-done | bytes 524320 | tf_op jit(solution)/shard_map/ppermute | solution.py:109
  62.8 0.8 constant_dynamic-update-slice_fusion.12
  63.6 1.5 %collective-permute-start.17 = (bf16[256,4096]{1,0:T(8,128)(2,1)}, bf16[256,4096]{1,0:T(8,128)(2,1)S(1)}, u32[]{:S(2)}, u32[]{:S(2)}) collective-permute-start(bf16[256,4096]{1,0:T(8,128)(2,1)} %constant_dynamic-update-slice_fusion.12), channel_id=1, source_target_pairs={{0,1},{1,0},{2,3},{3,2},{4,5},{5,4},{6,7},{7,6},{8,9},{9,8},{10,11... | collective-permute-start | bytes 6291464 | tf_op jit(solution)/shard_map/ppermute | solution.py:109
  65.1 0.8 constant_dynamic-update-slice_fusion.4
  66.0 2.4 %collective-permute-done.9 = bf16[64,4096]{1,0:T(8,128)(2,1)S(1)} collective-permute-done((bf16[64,4096]{1,0:T(8,128)(2,1)S(1)}, bf16[64,4096]{1,0:T(8,128)(2,1)S(1)}, u32[]{:S(2)}, u32[]{:S(2)}) %collective-permute-start.9) | collective-permute-done | bytes 524320 | tf_op jit(solution)/shard_map/ppermute | solution.py:109
  68.4 0.8 constant_dynamic-update-slice_fusion.3
  69.2 1.2 collective-permute-start.16
  70.5 1.3 fusion.49
  71.8 0.6 copy-done.2
  72.4 1.3 fusion.48
  73.7 1.3 fusion.53
  75.0 1.3 fusion.52
  76.2 0.6 copy-done.5
  76.8 1.3 fusion.51
  78.4 1.8 %fusion.4 = (f32[256]{0:T(256)S(1)}, f32[256]{0:T(256)S(1)}, f32[256]{0:T(256)S(1)}, f32[256]{0:T(256)S(1)}, bf16[256,384]{1,0:T(8,128)(2,1)S(1)}, /*index=5*/bf16[256,384]{1,0:T(8,128)(2,1)S(1)}, f32[256,384]{1,0:T(8,128)S(1)}) fusion(s32[384]{0:T(512)S(1)} %add_select_fusion, s32[256]{0:T(256)S(1)} %bitcast.85, f32[256,384]{1,0:T(8,128)S(1)} %fusion.48, ...), kind=kOutput, calls=%fused_computation.21 | convolution fusion | flops 809827328 | bytes 8009216 | tf_op jit(solution)/shard_map/dot_general | solution.py:172
  80.3 1.3 fusion.54
  81.5 1.4 %fusion.2 = bf16[256,4096]{1,0:T(8,128)(2,1)S(1)} fusion(f32[256,4096]{1,0:T(8,128)S(1)} %fusion.54, bf16[384,4096]{1,0:T(8,128)(2,1)S(1)} %bitcast.56, f32[256,384]{1,0:T(8,128)S(1)} %fusion.51, f32[256]{0:T(256)S(1)} %bitcast.74, f32[256]{0:T(256)S(1)} %bitcast.70, s32[384]{0:T(512)S(1)} %add_select_fusion, s32[256]{0:T(256)S(1)} %bitcast.66, ...), kind=kOutput, calls=%fused_computation.7 | convolution fusion | flops 808583168 | bytes 10229248 | tf_op jit(solution)/shard_map/dot_general | solution.py:200
  83.5 1.3 fusion.50
  84.8 1.4 %fusion.17 = f32[384,4096]{1,0:T(8,128)S(1)} fusion(bf16[256,4096]{1,0:T(8,128)(2,1)S(1)} %collective-permute-done.16, f32[256]{0:T(256)S(1)} %bitcast.75, f32[256]{0:T(256)S(1)} %bitcast.71, s32[384]{0:T(512)S(1)} %add_select_fusion, s32[256]{0:T(256)S(1)} %bitcast.67, s32[256]{0:T(256)S(1)} %bitcast.63, f32[256,384]{1,0:T(8,128)S(1)} %fusion.52, ...), kind=kOutput, calls=%fused_computation.43 | convolution fusion | flops 806486016 | bytes 9180672 | tf_op jit(solution)/shard_map/dot_general | solution.py:208
  86.2 2.9 %add_convert_fusion = bf16[384,4096]{1,0:T(8,128)(2,1)} fusion(f32[384,4096]{1,0:T(8,128)S(1)} %fusion.17, bf16[256,4096]{1,0:T(8,128)(2,1)S(1)} %copy-done.4, f32[256]{0:T(256)S(1)} %bitcast.82, f32[256]{0:T(256)S(1)} %bitcast.78, s32[384]{0:T(512)S(1)} %add_select_fusion, s32[256]{0:T(256)S(1)} %bitcast.90, s32[256]{0:T(256)S(1)} %bitcast.86, ...), kind=kOutput, calls=%fused_computation | convolution fusion | flops 809631744 | bytes 12326400 | tf_op jit(solution)/shard_map/dot_general | solution.py:208
  89.2 1.4 %add_convert_fusion.3 = bf16[256,4096]{1,0:T(8,128)(2,1)S(1)} fusion(bf16[256,4096]{1,0:T(8,128)(2,1)S(1)} %collective-permute-done.18, f32[256,4096]{1,0:T(8,128)S(1)} %fusion.50, bf16[384,4096]{1,0:T(8,128)(2,1)S(1)} %bitcast.57, f32[256,384]{1,0:T(8,128)S(1)} %get-tuple-element.33, f32[256]{0:T(256)S(1)} %bitcast.83, f32[256]{0:T(256)S(1)} %bitcast.79, ...), kind=kOutput, calls=%fused_computation.8 | convolution fusion | flops 812777472 | bytes 12326400 | tf_op jit(solution)/shard_map/dot_general | solution.py:200
  90.7 0.6 collective-permute-start.19
  91.3 1.2 fusion.43
  92.5 1.6 %collective-permute-start.24 = (f32[2,128]{1,0:T(2,128)S(1)}, f32[2,128]{1,0:T(2,128)S(1)}, u32[]{:S(2)}, u32[]{:S(2)}) collective-permute-start(f32[2,128]{1,0:T(2,128)S(1)} %split.73), channel_id=1, source_target_pairs={{0,16},{1,9},{2,18},{3,11},{4,20},{5,13},{6,22},{7,15},{8,24},{9,1... | collective-permute-start | bytes 3080 | tf_op jit(solution)/shard_map/ppermute | solution.py:109
  94.1 2.9 %add_convert_fusion.1 = bf16[384,4096]{1,0:T(8,128)(2,1)} fusion(f32[384,4096]{1,0:T(8,128)S(1)} %fusion.43, bf16[256,4096]{1,0:T(8,128)(2,1)S(1)} %copy-done.3, f32[256,384]{1,0:T(8,128)S(1)} %get-tuple-element.33, f32[256]{0:T(256)S(1)} %bitcast.84, f32[256]{0:T(256)S(1)} %bitcast.80, s32[384]{0:T(512)S(1)} %add_select_fusion, s32[256]{0:T(256)S(1)} %bitcast.92, ...), kind=kOutput, calls=%fused_computation.1 | convolution fusion | flops 809631744 | bytes 12326400 | tf_op jit(solution)/shard_map/dot_general | solution.py:208
  97.0 8.6 %collective-permute-done.24 = f32[2,128]{1,0:T(2,128)S(1)} collective-permute-done((f32[2,128]{1,0:T(2,128)S(1)}, f32[2,128]{1,0:T(2,128)S(1)}, u32[]{:S(2)}, u32[]{:S(2)}) %collective-permute-start.24) | collective-permute-done | bytes 1056 | tf_op jit(solution)/shard_map/ppermute | solution.py:109
  106.6 1.5 %collective-permute-start.20 = (bf16[64,4096]{1,0:T(8,128)(2,1)S(1)}, bf16[64,4096]{1,0:T(8,128)(2,1)S(1)}, u32[]{:S(2)}, u32[]{:S(2)}) collective-permute-start(bf16[64,4096]{1,0:T(8,128)(2,1)S(1)} %split.67), channel_id=1, source_target_pairs={{0,8},{1,17},{2,10},{3,19},{4,12},{5,21},{6,14},{7,23},{8,0},{9,25... | collective-permute-start | bytes 1572872 | tf_op jit(solution)/shard_map/ppermute | solution.py:109
  108.1 1.0 fusion.55
  109.3 1.9 %collective-permute-start.26 = (f32[2,32]{1,0:T(2,128)S(1)}, f32[2,32]{1,0:T(2,128)S(1)}, u32[]{:S(2)}, u32[]{:S(2)}) collective-permute-start(f32[2,32]{1,0:T(2,128)S(1)} %split.61), channel_id=1, source_target_pairs={{0,2},{1,3},{2,0},{3,1},{4,6},{5,7},{6,4},{7,5},{8,10},{9,11},{10,... | collective-permute-start | bytes 776 | tf_op jit(solution)/shard_map/ppermute | solution.py:109
  111.2 4.6 %collective-permute-done.20 = bf16[64,4096]{1,0:T(8,128)(2,1)S(1)} collective-permute-done((bf16[64,4096]{1,0:T(8,128)(2,1)S(1)}, bf16[64,4096]{1,0:T(8,128)(2,1)S(1)}, u32[]{:S(2)}, u32[]{:S(2)}) %collective-permute-start.20) | collective-permute-done | bytes 524320 | tf_op jit(solution)/shard_map/ppermute | solution.py:109
  116.0 1.9 %collective-permute-start.21 = (bf16[32,4096]{1,0:T(8,128)(2,1)S(1)}, bf16[32,4096]{1,0:T(8,128)(2,1)S(1)}, u32[]{:S(2)}, u32[]{:S(2)}) collective-permute-start(bf16[32,4096]{1,0:T(8,128)(2,1)S(1)} %split.69), channel_id=1, source_target_pairs={{0,2},{1,3},{2,0},{3,1},{4,6},{5,7},{6,4},{7,5},{8,10},{9,11},{10,... | collective-permute-start | bytes 786440 | tf_op jit(solution)/shard_map/ppermute | solution.py:109
  117.9 2.7 %add_convert_fusion.2 = bf16[384,4096]{1,0:T(8,128)(2,1)} fusion(f32[384,4096]{1,0:T(8,128)S(1)} %fusion.55, bf16[256,384]{1,0:T(8,128)(2,1)S(1)} %get-tuple-element.12, bf16[256,4096]{1,0:T(8,128)(2,1)S(1)} %copy-done.3), kind=kOutput, calls=%fused_computation.2 | convolution fusion | flops 808452096 | bytes 11730944 | tf_op jit(solution)/shard_map/dot_general | solution.py:208
  120.7 6.3 %collective-permute-start.27 = (f32[2,16]{1,0:T(2,128)S(1)}, f32[2,16]{1,0:T(2,128)S(1)}, u32[]{:S(2)}, u32[]{:S(2)}) collective-permute-start(f32[2,16]{1,0:T(2,128)S(1)} %split.63), channel_id=1, source_target_pairs={{0,4},{1,5},{2,6},{3,7},{4,0},{5,1},{6,2},{7,3},{8,12},{9,13},{10,... | collective-permute-start | bytes 392 | tf_op jit(solution)/shard_map/ppermute | solution.py:109
  127.0 1.9 %collective-permute-start.22 = (bf16[16,4096]{1,0:T(8,128)(2,1)S(1)}, bf16[16,4096]{1,0:T(8,128)(2,1)S(1)}, u32[]{:S(2)}, u32[]{:S(2)}) collective-permute-start(bf16[16,4096]{1,0:T(8,128)(2,1)S(1)} %split.71), channel_id=1, source_target_pairs={{0,4},{1,5},{2,6},{3,7},{4,0},{5,1},{6,2},{7,3},{8,12},{9,13},{10,... | collective-permute-start | bytes 393224 | tf_op jit(solution)/shard_map/ppermute | solution.py:109
  129.0 0.6 collective-permute-done.27
  130.2 4.2 %collective-permute-done.22 = bf16[16,4096]{1,0:T(8,128)(2,1)S(1)} collective-permute-done((bf16[16,4096]{1,0:T(8,128)(2,1)S(1)}, bf16[16,4096]{1,0:T(8,128)(2,1)S(1)}, u32[]{:S(2)}, u32[]{:S(2)}) %collective-permute-start.22) | collective-permute-done | bytes 131104 | tf_op jit(solution)/shard_map/ppermute | solution.py:109
  134.4 0.7 add_convert_fusion.7
  (65 shorter events, 5.6 us)
Async XLA Ops:
  0.6 69.9 %copy-start = (bf16[2,192,4096]{2,1,0:T(8,128)(2,1)S(1)}, bf16[2,192,4096]{2,1,0:T(8,128)(2,1)}, u32[]{:S(2)}) copy-start(bf16[2,192,4096]{2,1,0:T(8,128)(2,1)} %param.11) | copy-start | bytes 9437188
  2.3 7.0 %collective-permute-start = (f32[4,16]{1,0:T(4,128)S(1)}, f32[4,16]{1,0:T(4,128)S(1)}, u32[]{:S(2)}, u32[]{:S(2)}) collective-permute-start(f32[4,16]{1,0:T(4,128)S(1)} %maximum_bitcast_fusion), channel_id=1, source_target_pairs={{0,4},{1,5},{2,6},{3,7},{4,0},{5,1},{6,2},{7,3},{8,12},{9,13},{10,... | collective-permute-start | bytes 776 | tf_op jit(solution)/shard_map/ppermute | solution.py:109
  6.4 15.0 %collective-permute-start.10 = (bf16[16,4096]{1,0:T(8,128)(2,1)}, bf16[16,4096]{1,0:T(8,128)(2,1)S(1)}, u32[]{:S(2)}, u32[]{:S(2)}) collective-permute-start(bf16[16,4096]{1,0:T(8,128)(2,1)} %param.7), channel_id=1, source_target_pairs={{0,4},{1,5},{2,6},{3,7},{4,0},{5,1},{6,2},{7,3},{8,12},{9,13},{10,... | collective-permute-start | bytes 393224 | tf_op jit(solution)/shard_map/ppermute | solution.py:109
  6.5 17.8 %collective-permute-start.5 = (bf16[16,4096]{1,0:T(8,128)(2,1)}, bf16[16,4096]{1,0:T(8,128)(2,1)S(1)}, u32[]{:S(2)}, u32[]{:S(2)}) collective-permute-start(bf16[16,4096]{1,0:T(8,128)(2,1)} %param.8), channel_id=1, source_target_pairs={{0,4},{1,5},{2,6},{3,7},{4,0},{5,1},{6,2},{7,3},{8,12},{9,13},{10,... | collective-permute-start | bytes 393224 | tf_op jit(solution)/shard_map/ppermute | solution.py:109
  9.4 3.6 %collective-permute-start.1 = (f32[4,32]{1,0:T(4,128)S(1)}, f32[4,32]{1,0:T(4,128)S(1)}, u32[]{:S(2)}, u32[]{:S(2)}) collective-permute-start(f32[4,32]{1,0:T(4,128)S(1)} %pad_maximum_fusion.2), channel_id=1, source_target_pairs={{0,2},{1,3},{2,0},{3,1},{4,6},{5,7},{6,4},{7,5},{8,10},{9,11},{10,... | collective-permute-start | bytes 1544 | tf_op jit(solution)/shard_map/ppermute | solution.py:109
  13.1 4.6 %collective-permute-start.2 = (f32[4,64]{1,0:T(4,128)S(1)}, f32[4,64]{1,0:T(4,128)S(1)}, u32[]{:S(2)}, u32[]{:S(2)}) collective-permute-start(f32[4,64]{1,0:T(4,128)S(1)} %pad_maximum_fusion.3), channel_id=1, source_target_pairs={{0,8},{1,17},{2,10},{3,19},{4,12},{5,21},{6,14},{7,23},{8,0},{9,25... | collective-permute-start | bytes 3080 | tf_op jit(solution)/shard_map/ppermute | solution.py:109
  16.2 3.6 %collective-permute-start.3 = (f32[4,64]{1,0:T(4,128)S(1)}, f32[4,64]{1,0:T(4,128)S(1)}, u32[]{:S(2)}, u32[]{:S(2)}) collective-permute-start(f32[4,64]{1,0:T(4,128)S(1)} %pad_maximum_fusion.3), channel_id=1, source_target_pairs={{0,16},{1,9},{2,18},{3,11},{4,20},{5,13},{6,22},{7,15},{8,24},{9,1... | collective-permute-start | bytes 3080 | tf_op jit(solution)/shard_map/ppermute | solution.py:109
  17.7 3.6 %collective-permute-start.4 = (f32[4,64]{1,0:T(4,128)S(1)}, f32[4,64]{1,0:T(4,128)S(1)}, u32[]{:S(2)}, u32[]{:S(2)}) collective-permute-start(f32[4,64]{1,0:T(4,128)S(1)} %collective-permute-done.2), channel_id=1, source_target_pairs={{0,16},{1,9},{2,18},{3,11},{4,20},{5,13},{6,22},{7,15},{8,24},{9,1... | collective-permute-start | bytes 3080 | tf_op jit(solution)/shard_map/ppermute | solution.py:109
  21.4 49.1 %collective-permute-start.15 = (f32[4,256]{1,0:T(4,128)S(1)}, f32[4,256]{1,0:T(4,128)S(1)}, u32[]{:S(2)}, u32[]{:S(2)}) collective-permute-start(f32[4,256]{1,0:T(4,128)S(1)} %concatenate.39), channel_id=1, source_target_pairs={{0,1},{1,0},{2,3},{3,2},{4,5},{5,4},{6,7},{7,6},{8,9},{9,8},{10,11... | collective-permute-start | bytes 12296 | tf_op jit(solution)/shard_map/ppermute | solution.py:109
  22.3 9.2 %collective-permute-start.11 = (bf16[32,4096]{1,0:T(8,128)(2,1)S(1)}, bf16[32,4096]{1,0:T(8,128)(2,1)S(1)}, u32[]{:S(2)}, u32[]{:S(2)}) collective-permute-start(bf16[32,4096]{1,0:T(8,128)(2,1)S(1)} %pad_maximum_fusion.1), channel_id=1, source_target_pairs={{0,2},{1,3},{2,0},{3,1},{4,6},{5,7},{6,4},{7,5},{8,10},{9,11},{10,... | collective-permute-start | bytes 786440 | tf_op jit(solution)/shard_map/ppermute | solution.py:109
  25.2 11.7 %collective-permute-start.6 = (bf16[32,4096]{1,0:T(8,128)(2,1)S(1)}, bf16[32,4096]{1,0:T(8,128)(2,1)S(1)}, u32[]{:S(2)}, u32[]{:S(2)}) collective-permute-start(bf16[32,4096]{1,0:T(8,128)(2,1)S(1)} %pad_maximum_fusion), channel_id=1, source_target_pairs={{0,2},{1,3},{2,0},{3,1},{4,6},{5,7},{6,4},{7,5},{8,10},{9,11},{10,... | collective-permute-start | bytes 786440 | tf_op jit(solution)/shard_map/ppermute | solution.py:109
  32.3 10.5 %collective-permute-start.12 = (bf16[64,4096]{1,0:T(8,128)(2,1)}, bf16[64,4096]{1,0:T(8,128)(2,1)S(1)}, u32[]{:S(2)}, u32[]{:S(2)}) collective-permute-start(bf16[64,4096]{1,0:T(8,128)(2,1)} %get-tuple-element.15), channel_id=1, source_target_pairs={{0,8},{1,17},{2,10},{3,19},{4,12},{5,21},{6,14},{7,23},{8,0},{9,25... | collective-permute-start | bytes 1572872 | tf_op jit(solution)/shard_map/ppermute | solution.py:109
  37.7 16.4 %collective-permute-start.7 = (bf16[64,4096]{1,0:T(8,128)(2,1)}, bf16[64,4096]{1,0:T(8,128)(2,1)S(1)}, u32[]{:S(2)}, u32[]{:S(2)}) collective-permute-start(bf16[64,4096]{1,0:T(8,128)(2,1)} %get-tuple-element.13), channel_id=1, source_target_pairs={{0,8},{1,17},{2,10},{3,19},{4,12},{5,21},{6,14},{7,23},{8,0},{9,25... | collective-permute-start | bytes 1572872 | tf_op jit(solution)/shard_map/ppermute | solution.py:109
  38.2 16.7 %collective-permute-start.13 = (bf16[64,4096]{1,0:T(8,128)(2,1)}, bf16[64,4096]{1,0:T(8,128)(2,1)S(1)}, u32[]{:S(2)}, u32[]{:S(2)}) collective-permute-start(bf16[64,4096]{1,0:T(8,128)(2,1)} %get-tuple-element.15), channel_id=1, source_target_pairs={{0,16},{1,9},{2,18},{3,11},{4,20},{5,13},{6,22},{7,15},{8,24},{9,1... | collective-permute-start | bytes 1572872 | tf_op jit(solution)/shard_map/ppermute | solution.py:109
  39.6 25.5 %collective-permute-start.8 = (bf16[64,4096]{1,0:T(8,128)(2,1)}, bf16[64,4096]{1,0:T(8,128)(2,1)S(1)}, u32[]{:S(2)}, u32[]{:S(2)}) collective-permute-start(bf16[64,4096]{1,0:T(8,128)(2,1)} %get-tuple-element.13), channel_id=1, source_target_pairs={{0,16},{1,9},{2,18},{3,11},{4,20},{5,13},{6,22},{7,15},{8,24},{9,1... | collective-permute-start | bytes 1572872 | tf_op jit(solution)/shard_map/ppermute | solution.py:109
  42.8 20.0 %collective-permute-start.14 = (bf16[64,4096]{1,0:T(8,128)(2,1)S(1)}, bf16[64,4096]{1,0:T(8,128)(2,1)S(1)}, u32[]{:S(2)}, u32[]{:S(2)}) collective-permute-start(bf16[64,4096]{1,0:T(8,128)(2,1)S(1)} %collective-permute-done.12), channel_id=1, source_target_pairs={{0,16},{1,9},{2,18},{3,11},{4,20},{5,13},{6,22},{7,15},{8,24},{9,1... | collective-permute-start | bytes 1572872 | tf_op jit(solution)/shard_map/ppermute | solution.py:109
  54.0 14.4 %collective-permute-start.9 = (bf16[64,4096]{1,0:T(8,128)(2,1)S(1)}, bf16[64,4096]{1,0:T(8,128)(2,1)S(1)}, u32[]{:S(2)}, u32[]{:S(2)}) collective-permute-start(bf16[64,4096]{1,0:T(8,128)(2,1)S(1)} %collective-permute-done.7), channel_id=1, source_target_pairs={{0,16},{1,9},{2,18},{3,11},{4,20},{5,13},{6,22},{7,15},{8,24},{9,1... | collective-permute-start | bytes 1572872 | tf_op jit(solution)/shard_map/ppermute | solution.py:109
  63.6 6.9 %copy-start.3 = (bf16[256,4096]{1,0:T(8,128)(2,1)S(1)}, bf16[256,4096]{1,0:T(8,128)(2,1)}, u32[]{:S(2)}) copy-start(bf16[256,4096]{1,0:T(8,128)(2,1)} %constant_dynamic-update-slice_fusion.12) | copy-start | bytes 6291460
  63.6 10.1 %collective-permute-start.17 = (bf16[256,4096]{1,0:T(8,128)(2,1)}, bf16[256,4096]{1,0:T(8,128)(2,1)S(1)}, u32[]{:S(2)}, u32[]{:S(2)}) collective-permute-start(bf16[256,4096]{1,0:T(8,128)(2,1)} %constant_dynamic-update-slice_fusion.12), channel_id=1, source_target_pairs={{0,1},{1,0},{2,3},{3,2},{4,5},{5,4},{6,7},{7,6},{8,9},{9,8},{10,11... | collective-permute-start | bytes 6291464 | tf_op jit(solution)/shard_map/ppermute | solution.py:109
  69.2 7.0 %collective-permute-start.16 = (bf16[256,4096]{1,0:T(8,128)(2,1)}, bf16[256,4096]{1,0:T(8,128)(2,1)S(1)}, u32[]{:S(2)}, u32[]{:S(2)}) collective-permute-start(bf16[256,4096]{1,0:T(8,128)(2,1)} %constant_dynamic-update-slice_fusion.3), channel_id=1, source_target_pairs={{0,1},{1,0},{2,3},{3,2},{4,5},{5,4},{6,7},{7,6},{8,9},{9,8},{10,11... | collective-permute-start | bytes 6291464 | tf_op jit(solution)/shard_map/ppermute | solution.py:109
  70.5 1.9 %copy-start.2 = (bf16[2,192,4096]{2,1,0:T(8,128)(2,1)S(1)}, bf16[2,192,4096]{2,1,0:T(8,128)(2,1)}, u32[]{:S(2)}) copy-start(bf16[2,192,4096]{2,1,0:T(8,128)(2,1)} %param.12) | copy-start | bytes 9437188
  74.9 1.9 %copy-start.5 = (bf16[2,192,4096]{2,1,0:T(8,128)(2,1)S(1)}, bf16[2,192,4096]{2,1,0:T(8,128)(2,1)}, u32[]{:S(2)}) copy-start(bf16[2,192,4096]{2,1,0:T(8,128)(2,1)} %param.13) | copy-start | bytes 9437188
  76.8 1.6 %copy-start.4 = (bf16[256,4096]{1,0:T(8,128)(2,1)S(1)}, bf16[256,4096]{1,0:T(8,128)(2,1)}, u32[]{:S(2)}) copy-start(bf16[256,4096]{1,0:T(8,128)(2,1)} %constant_dynamic-update-slice_fusion.3) | copy-start | bytes 6291460
  83.0 6.2 %collective-permute-start.18 = (bf16[256,4096]{1,0:T(8,128)(2,1)S(1)}, bf16[256,4096]{1,0:T(8,128)(2,1)S(1)}, u32[]{:S(2)}, u32[]{:S(2)}) collective-permute-start(bf16[256,4096]{1,0:T(8,128)(2,1)S(1)} %fusion.2), channel_id=1, source_target_pairs={{0,1},{1,0},{2,3},{3,2},{4,5},{5,4},{6,7},{7,6},{8,9},{9,8},{10,11... | collective-permute-start | bytes 6291464 | tf_op jit(solution)/shard_map/ppermute | solution.py:109
  83.0 9.5 %collective-permute-start.23 = (f32[2,256]{1,0:T(2,128)S(1)}, f32[2,256]{1,0:T(2,128)S(1)}, u32[]{:S(2)}, u32[]{:S(2)}) collective-permute-start(f32[2,256]{1,0:T(2,128)S(1)} %pad_maximum_fusion.4), channel_id=1, source_target_pairs={{0,1},{1,0},{2,3},{3,2},{4,5},{5,4},{6,7},{7,6},{8,9},{9,8},{10,11... | collective-permute-start | bytes 6152 | tf_op jit(solution)/shard_map/ppermute | solution.py:109
  90.7 15.5 %collective-permute-start.19 = (bf16[128,4096]{1,0:T(8,128)(2,1)S(1)}, bf16[128,4096]{1,0:T(8,128)(2,1)S(1)}, u32[]{:S(2)}, u32[]{:S(2)}) collective-permute-start(bf16[128,4096]{1,0:T(8,128)(2,1)S(1)} %split.65), channel_id=1, source_target_pairs={{0,16},{1,9},{2,18},{3,11},{4,20},{5,13},{6,22},{7,15},{8,24},{9,1... | collective-permute-start | bytes 3145736 | tf_op jit(solution)/shard_map/ppermute | solution.py:109
  92.5 13.1 %collective-permute-start.24 = (f32[2,128]{1,0:T(2,128)S(1)}, f32[2,128]{1,0:T(2,128)S(1)}, u32[]{:S(2)}, u32[]{:S(2)}) collective-permute-start(f32[2,128]{1,0:T(2,128)S(1)} %split.73), channel_id=1, source_target_pairs={{0,16},{1,9},{2,18},{3,11},{4,20},{5,13},{6,22},{7,15},{8,24},{9,1... | collective-permute-start | bytes 3080 | tf_op jit(solution)/shard_map/ppermute | solution.py:109
  105.7 3.6 %collective-permute-start.25 = (f32[2,64]{1,0:T(2,128)S(1)}, f32[2,64]{1,0:T(2,128)S(1)}, u32[]{:S(2)}, u32[]{:S(2)}) collective-permute-start(f32[2,64]{1,0:T(2,128)S(1)} %split.59), channel_id=1, source_target_pairs={{0,8},{1,17},{2,10},{3,19},{4,12},{5,21},{6,14},{7,23},{8,0},{9,25... | collective-permute-start | bytes 1544 | tf_op jit(solution)/shard_map/ppermute | solution.py:109
  106.6 9.2 %collective-permute-start.20 = (bf16[64,4096]{1,0:T(8,128)(2,1)S(1)}, bf16[64,4096]{1,0:T(8,128)(2,1)S(1)}, u32[]{:S(2)}, u32[]{:S(2)}) collective-permute-start(bf16[64,4096]{1,0:T(8,128)(2,1)S(1)} %split.67), channel_id=1, source_target_pairs={{0,8},{1,17},{2,10},{3,19},{4,12},{5,21},{6,14},{7,23},{8,0},{9,25... | collective-permute-start | bytes 1572872 | tf_op jit(solution)/shard_map/ppermute | solution.py:109
  109.3 11.3 %collective-permute-start.26 = (f32[2,32]{1,0:T(2,128)S(1)}, f32[2,32]{1,0:T(2,128)S(1)}, u32[]{:S(2)}, u32[]{:S(2)}) collective-permute-start(f32[2,32]{1,0:T(2,128)S(1)} %split.61), channel_id=1, source_target_pairs={{0,2},{1,3},{2,0},{3,1},{4,6},{5,7},{6,4},{7,5},{8,10},{9,11},{10,... | collective-permute-start | bytes 776 | tf_op jit(solution)/shard_map/ppermute | solution.py:109
  116.0 11.0 %collective-permute-start.21 = (bf16[32,4096]{1,0:T(8,128)(2,1)S(1)}, bf16[32,4096]{1,0:T(8,128)(2,1)S(1)}, u32[]{:S(2)}, u32[]{:S(2)}) collective-permute-start(bf16[32,4096]{1,0:T(8,128)(2,1)S(1)} %split.69), channel_id=1, source_target_pairs={{0,2},{1,3},{2,0},{3,1},{4,6},{5,7},{6,4},{7,5},{8,10},{9,11},{10,... | collective-permute-start | bytes 786440 | tf_op jit(solution)/shard_map/ppermute | solution.py:109
  117.9 17.2 %copy-start.1 = (bf16[2,192,4096]{2,1,0:T(8,128)(2,1)S(1)}, bf16[2,192,4096]{2,1,0:T(8,128)(2,1)}, u32[]{:S(2)}) copy-start(bf16[2,192,4096]{2,1,0:T(8,128)(2,1)} %param.11) | copy-start | bytes 9437188
  120.7 8.9 %collective-permute-start.27 = (f32[2,16]{1,0:T(2,128)S(1)}, f32[2,16]{1,0:T(2,128)S(1)}, u32[]{:S(2)}, u32[]{:S(2)}) collective-permute-start(f32[2,16]{1,0:T(2,128)S(1)} %split.63), channel_id=1, source_target_pairs={{0,4},{1,5},{2,6},{3,7},{4,0},{5,1},{6,2},{7,3},{8,12},{9,13},{10,... | collective-permute-start | bytes 392 | tf_op jit(solution)/shard_map/ppermute | solution.py:109
  127.0 7.3 %collective-permute-start.22 = (bf16[16,4096]{1,0:T(8,128)(2,1)S(1)}, bf16[16,4096]{1,0:T(8,128)(2,1)S(1)}, u32[]{:S(2)}, u32[]{:S(2)}) collective-permute-start(bf16[16,4096]{1,0:T(8,128)(2,1)S(1)} %split.71), channel_id=1, source_target_pairs={{0,4},{1,5},{2,6},{3,7},{4,0},{5,1},{6,2},{7,3},{8,12},{9,13},{10,... | collective-permute-start | bytes 393224 | tf_op jit(solution)/shard_map/ppermute | solution.py:109

commit v2 on v1

--- a/solution.py
+++ b/solution.py
@@ -129,8 +129,7 @@
     pieces = [block]
     for masks in across:
         pieces = pieces + [swap(piece, masks) for piece in pieces]
-    half = jnp.concatenate(pieces, axis=axis)
-    return half, swap(half, (1, 1))
+    return pieces
 
 
 def hand_out(half, other, axis):
@@ -150,12 +149,18 @@
     model_width = tokens.shape[1]
     chosen = routes.shape[1]
     local_experts, part, _ = gate_weight.shape
-    side = jnp.concatenate(
-        [gate_values.astype(jnp.float32), routes.astype(jnp.float32)], axis=1
-    ).T
-    sides = collect(side, 1)
-    xs = collect(tokens, 0)
-    dys = collect(grad_out, 0)
+    side = jnp.concatenate([gate_values, routes.astype(jnp.bfloat16)], axis=1)
+    side = jnp.pad(side, ((0, 0), (0, 128 - 2 * chosen)))
+    x_pieces = collect(jnp.concatenate([tokens, side], axis=1), 0)
+    dy_pieces = collect(grad_out, 0)
+
+    def both_cores(pieces):
+        half = jnp.concatenate(pieces, axis=0)
+        return half, swap(half, (1, 1))
+
+    sides = both_cores([piece[:, model_width:] for piece in x_pieces])
+    xs = both_cores([piece[:, :model_width] for piece in x_pieces])
+    dys = both_cores(dy_pieces)
     gate_mat = gate_weight.reshape(local_experts * part, model_width)
     up_mat = up_weight.reshape(local_experts * part, model_width)
     down_mat = down_weight.reshape(local_experts * part, model_width)
@@ -164,9 +169,8 @@
     unit_expert = lax.broadcasted_iota(jnp.int32, (1, local_experts * part), 1) // part
     input_parts, gate_parts, lefts = [], [], []
     for x, dy, info in zip(xs, dys, sides):
-        info = info.T
-        gates = info[:, :chosen]
-        named = info[:, chosen:].astype(jnp.int32) - lax.axis_index("expert") * local_experts
+        gates = info[:, :chosen].astype(jnp.float32)
+        named = info[:, chosen : 2 * chosen].astype(jnp.int32) - lax.axis_index("expert") * local_experts
         gate_pre = lax.dot_general(x, gate_mat, over_width, preferred_element_type=jnp.float32)
         up_pre = lax.dot_general(x, up_mat, over_width, preferred_element_type=jnp.float32)
         back_hidden = lax.dot_general(

time: 135 us -> 126 us (0.933)
  local copies, waits for them, and re-layouts: 13.3 us -> 5.35 us
  starting transfers between devices: 36.9 us -> 31.5 us
  waiting for transfers between devices: 52.7 us -> 54.7 us
  other arithmetic: 5.39 us -> 6.91 us
    unnamed x20 -> x17, local copies, waits for them, and re-layouts: 9.53 us -> 3.15 us
    ppermute x28 -> x23, starting transfers between devices: 36.9 us -> 31.5 us  [swap(): return lax.ppermute(values, ('expert', 'dp'), pairs)]
    concatenate x0 -> x4, other arithmetic: none -> 2.4 us  [the longest x1 1.57 us: all_tokens(): x_pieces = collect(jnp.concatenate([tokens, side], axis=1), 0)]
    ppermute x28 -> x23, waiting for transfers between devices: 52.7 us -> 54.7 us  [swap(): return lax.ppermute(values, ('expert', 'dp'), pairs)]
    concatenate x3 -> x1, local copies, waits for them, and re-layouts: 1.76 us -> 0.03 us  [both_cores(): half = jnp.concatenate(pieces, axis=0)]
  transfers between devices with their start and end apart: 28 -> 23, of which waited for: 14 -> 12; matrix products, arithmetic and copies ran while one was open for 26% -> 24% of each run, Pallas kernels for 0% -> 0%
where the time goes in v2:
time: 126 us; the launch traced here: 125 us
  waiting for transfers between devices  54.7 us (43%)
  starting transfers between devices  31.5 us (25%)
  matrix products  25.9 us (21%)
  other arithmetic  6.91 us (5%)
  local copies, waits for them, and re-layouts  5.35 us (4%)
    ppermute x23, waiting for transfers between devices, swap(): return lax.ppermute(values, ('expert', 'dp'), pairs)  54.7 us
    ppermute x23, starting transfers between devices, swap(): return lax.ppermute(values, ('expert', 'dp'), pairs)  31.5 us
    dot_general x6, matrix products, all_tokens(): lax.dot_general(lefts[i][left], right[i], over_rows, preferred_element_ty...  12.3 us
    unnamed x17, local copies, waits for them, and re-layouts  3.15 us
    dot_general x2, matrix products, all_tokens(): lax.dot_general(dy, down_mat, over_width, preferred_element_type=jnp.floa...  3.1 us
    dot_general x2, matrix products, all_tokens(): jnp.dot(grad_up_pre, up_mat, preferred_element_type=jnp.float32)  2.92 us
    dot_general x2, matrix products, all_tokens(): jnp.dot(grad_gate_pre, gate_mat, preferred_element_type=jnp.float32)  2.54 us
    dot_general x2, matrix products, all_tokens(): lax.dot_general(x, gate_mat, over_width, preferred_element_type=jnp.float32)  2.53 us
  transfers between devices with their start and end apart: 23, of which 12 were waited for; matrix products, arithmetic and copies ran while one was open for 24% of the time, Pallas kernels for 0%

profile of v2, /device:TPU:0, one launch (start us, length us, event | category | flops | bytes accessed | tf_op | source)
XLA Modules:
  0.0 125.4 jit_solution(15748271069954801871)
XLA Ops:
  0.7 4.1 %collective-permute-start.5 = (bf16[16,4096]{1,0:T(8,128)(2,1)}, bf16[16,4096]{1,0:T(8,128)(2,1)S(1)}, u32[]{:S(2)}, u32[]{:S(2)}) collective-permute-start(bf16[16,4096]{1,0:T(8,128)(2,1)} %param.8), channel_id=1, source_target_pairs={{0,4},{1,5},{2,6},{3,7},{4,0},{5,1},{6,2},{7,3},{8,12},{9,13},{10,... | collective-permute-start | bytes 393224 | tf_op jit(solution)/shard_map/ppermute | solution.py:109
  4.8 0.7 convert_element_type.95
  5.4 0.7 pad_maximum_fusion.7
  6.2 1.6 %pad_maximum_fusion.4 = bf16[16,4224]{1,0:T(8,128)(2,1)} fusion(bf16[16,128]{1,0:T(8,128)(2,1)S(1)} %pad.4.clone, bf16[16,4096]{1,0:T(8,128)(2,1)} %param.7), kind=kLoop, calls=%fused_computation.58 | loop fusion | flops 270336 | bytes 270336 | tf_op jit(solution)/shard_map/concatenate | solution.py:154
  7.8 0.3 collective-permute-start
  8.0 1.6 %constant_dynamic-update-slice_fusion.2 = (bf16[64,4096]{1,0:T(8,128)(2,1)}, bf16[256,4096]{1,0:T(8,128)(2,1)}) fusion(bf16[16,4096]{1,0:T(8,128)(2,1)} %param.8), kind=kLoop, calls=%fused_computation.76 | loop fusion | bytes 393216
  9.7 1.8 %collective-permute-done.5 = bf16[16,4096]{1,0:T(8,128)(2,1)S(1)} collective-permute-done((bf16[16,4096]{1,0:T(8,128)(2,1)}, bf16[16,4096]{1,0:T(8,128)(2,1)S(1)}, u32[]{:S(2)}, u32[]{:S(2)}) %collective-permute-start.5) | collective-permute-done | bytes 131104 | tf_op jit(solution)/shard_map/ppermute | solution.py:109
  11.4 0.9 pad_maximum_fusion.3
  12.4 3.7 %collective-permute-start.6 = (bf16[32,4096]{1,0:T(8,128)(2,1)S(1)}, bf16[32,4096]{1,0:T(8,128)(2,1)S(1)}, u32[]{:S(2)}, u32[]{:S(2)}) collective-permute-start(bf16[32,4096]{1,0:T(8,128)(2,1)S(1)} %pad_maximum_fusion.3), channel_id=1, source_target_pairs={{0,2},{1,3},{2,0},{3,1},{4,6},{5,7},{6,4},{7,5},{8,10},{9,11},{10,... | collective-permute-start | bytes 786440 | tf_op jit(solution)/shard_map/ppermute | solution.py:109
  16.1 0.7 constant_dynamic-update-slice_fusion.1
  16.8 0.3 collective-permute-done
  17.1 0.9 pad_maximum_fusion.2
  18.0 0.9 collective-permute-start.1
  18.9 4.3 %collective-permute-done.6 = bf16[32,4096]{1,0:T(8,128)(2,1)S(1)} collective-permute-done((bf16[32,4096]{1,0:T(8,128)(2,1)S(1)}, bf16[32,4096]{1,0:T(8,128)(2,1)S(1)}, u32[]{:S(2)}, u32[]{:S(2)}) %collective-permute-start.6) | collective-permute-done | bytes 262176 | tf_op jit(solution)/shard_map/ppermute | solution.py:109
  23.2 0.8 constant_dynamic-update-slice_fusion
  24.0 1.5 %collective-permute-start.8 = (bf16[64,4096]{1,0:T(8,128)(2,1)}, bf16[64,4096]{1,0:T(8,128)(2,1)S(1)}, u32[]{:S(2)}, u32[]{:S(2)}) collective-permute-start(bf16[64,4096]{1,0:T(8,128)(2,1)} %get-tuple-element.21), channel_id=1, source_target_pairs={{0,16},{1,9},{2,18},{3,11},{4,20},{5,13},{6,22},{7,15},{8,24},{9,1... | collective-permute-start | bytes 1572872 | tf_op jit(solution)/shard_map/ppermute | solution.py:109
  25.6 1.5 %collective-permute-start.7 = (bf16[64,4096]{1,0:T(8,128)(2,1)}, bf16[64,4096]{1,0:T(8,128)(2,1)S(1)}, u32[]{:S(2)}, u32[]{:S(2)}) collective-permute-start(bf16[64,4096]{1,0:T(8,128)(2,1)} %get-tuple-element.21), channel_id=1, source_target_pairs={{0,8},{1,17},{2,10},{3,19},{4,12},{5,21},{6,14},{7,23},{8,0},{9,25... | collective-permute-start | bytes 1572872 | tf_op jit(solution)/shard_map/ppermute | solution.py:109
  27.0 1.4 %collective-permute-done.1 = bf16[32,4224]{1,0:T(8,128)(2,1)S(1)} collective-permute-done((bf16[32,4224]{1,0:T(8,128)(2,1)S(1)}, bf16[32,4224]{1,0:T(8,128)(2,1)S(1)}, u32[]{:S(2)}, u32[]{:S(2)}) %collective-permute-start.1) | collective-permute-done | bytes 270368 | tf_op jit(solution)/shard_map/ppermute | solution.py:109
  28.5 1.6 %collective-permute-start.2 = (bf16[64,4224]{1,0:T(8,128)(2,1)S(1)}, bf16[64,4224]{1,0:T(8,128)(2,1)S(1)}, u32[]{:S(2)}, u32[]{:S(2)}) collective-permute-start(bf16[64,4224]{1,0:T(8,128)(2,1)S(1)} %pad_maximum_fusion.1), channel_id=1, source_target_pairs={{0,8},{1,17},{2,10},{3,19},{4,12},{5,21},{6,14},{7,23},{8,0},{9,25... | collective-permute-start | bytes 1622024 | tf_op jit(solution)/shard_map/ppermute | solution.py:109
  30.2 1.6 %collective-permute-start.3 = (bf16[64,4224]{1,0:T(8,128)(2,1)S(1)}, bf16[64,4224]{1,0:T(8,128)(2,1)S(1)}, u32[]{:S(2)}, u32[]{:S(2)}) collective-permute-start(bf16[64,4224]{1,0:T(8,128)(2,1)S(1)} %pad_maximum_fusion.1), channel_id=1, source_target_pairs={{0,16},{1,9},{2,18},{3,11},{4,20},{5,13},{6,22},{7,15},{8,24},{9,1... | collective-permute-start | bytes 1622024 | tf_op jit(solution)/shard_map/ppermute | solution.py:109
  31.8 8.9 %collective-permute-done.7 = bf16[64,4096]{1,0:T(8,128)(2,1)S(1)} collective-permute-done((bf16[64,4096]{1,0:T(8,128)(2,1)}, bf16[64,4096]{1,0:T(8,128)(2,1)S(1)}, u32[]{:S(2)}, u32[]{:S(2)}) %collective-permute-start.7) | collective-permute-done | bytes 524320 | tf_op jit(solution)/shard_map/ppermute | solution.py:109
  40.6 0.5 collective-permute-start.9
  41.2 11.0 %collective-permute-done.2 = bf16[64,4224]{1,0:T(8,128)(2,1)S(1)} collective-permute-done((bf16[64,4224]{1,0:T(8,128)(2,1)S(1)}, bf16[64,4224]{1,0:T(8,128)(2,1)S(1)}, u32[]{:S(2)}, u32[]{:S(2)}) %collective-permute-start.2) | collective-permute-done | bytes 540704 | tf_op jit(solution)/shard_map/ppermute | solution.py:109
  52.2 0.5 collective-permute-start.4
  52.9 2.8 %collective-permute-done.9 = bf16[64,4096]{1,0:T(8,128)(2,1)S(1)} collective-permute-done((bf16[64,4096]{1,0:T(8,128)(2,1)S(1)}, bf16[64,4096]{1,0:T(8,128)(2,1)S(1)}, u32[]{:S(2)}, u32[]{:S(2)}) %collective-permute-start.9) | collective-permute-done | bytes 524320 | tf_op jit(solution)/shard_map/ppermute | solution.py:109
  55.8 5.8 %collective-permute-done.4 = bf16[64,4224]{1,0:T(8,128)(2,1)S(1)} collective-permute-done((bf16[64,4224]{1,0:T(8,128)(2,1)S(1)}, bf16[64,4224]{1,0:T(8,128)(2,1)S(1)}, u32[]{:S(2)}, u32[]{:S(2)}) %collective-permute-start.4) | collective-permute-done | bytes 540704 | tf_op jit(solution)/shard_map/ppermute | solution.py:109
  61.9 0.6 collective-permute-start.12
  62.6 0.2 slice_reduce_fusion.7
  62.8 1.3 %fusion.43 = f32[256,384]{1,0:T(8,128)S(1)} fusion(bf16[256,4096]{1,0:T(8,128)(2,1)S(1)} %pad_maximum_fusion, bf16[384,4096]{1,0:T(8,128)(2,1)S(1)} %bitcast.38), kind=kOutput, calls=%fused_computation.101 | convolution fusion | flops 805306368 | bytes 5636096 | tf_op jit(solution)/shard_map/dot_general | solution.py:174
  64.1 0.6 copy-done.2
  64.7 1.3 %fusion.42 = f32[256,384]{1,0:T(8,128)S(1)} fusion(bf16[256,4096]{1,0:T(8,128)(2,1)S(1)} %pad_maximum_fusion, bf16[384,4096]{1,0:T(8,128)(2,1)S(1)} %bitcast.42), kind=kOutput, calls=%fused_computation.100 | convolution fusion | flops 805306368 | bytes 5636096 | tf_op jit(solution)/shard_map/dot_general | solution.py:175
  65.9 0.2 slice_reduce_fusion.6
  66.2 0.2 slice_reduce_fusion.2
  66.5 0.2 slice_reduce_fusion.3
  66.7 1.3 %fusion.45 = f32[256,384]{1,0:T(8,128)S(1)} fusion(bf16[256,4096]{1,0:T(8,128)(2,1)S(1)} %collective-permute-done.11, bf16[384,4096]{1,0:T(8,128)(2,1)S(1)} %bitcast.53), kind=kOutput, calls=%fused_computation.103 | convolution fusion | flops 805306368 | bytes 5636096 | tf_op jit(solution)/shard_map/dot_general | solution.py:176
  68.0 1.3 %fusion.47 = f32[256,384]{1,0:T(8,128)S(1)} fusion(bf16[256,4096]{1,0:T(8,128)(2,1)S(1)} %collective-permute-done.12, bf16[384,4096]{1,0:T(8,128)(2,1)S(1)} %bitcast.40), kind=kOutput, calls=%fused_computation.105 | convolution fusion | flops 805306368 | bytes 5636096 | tf_op jit(solution)/shard_map/dot_general | solution.py:174
  69.2 1.3 %fusion.46 = f32[256,384]{1,0:T(8,128)S(1)} fusion(bf16[256,4096]{1,0:T(8,128)(2,1)S(1)} %collective-permute-done.12, bf16[384,4096]{1,0:T(8,128)(2,1)S(1)} %bitcast.43), kind=kOutput, calls=%fused_computation.104 | convolution fusion | flops 805306368 | bytes 5636096 | tf_op jit(solution)/shard_map/dot_general | solution.py:175
  70.5 1.8 %fusion.4 = (f32[256]{0:T(256)S(1)}, f32[256]{0:T(256)S(1)}, f32[256]{0:T(256)S(1)}, f32[256]{0:T(256)S(1)}, bf16[256,384]{1,0:T(8,128)(2,1)S(1)}, /*index=5*/bf16[256,384]{1,0:T(8,128)(2,1)S(1)}, f32[256,384]{1,0:T(8,128)S(1)}) fusion(s32[384]{0:T(512)S(1)} %add_select_fusion, s32[256]{0:T(256)S(1)} %get-tuple-element.9, f32[256,384]{1,0:T(8,128)S(1)} %fusion.42, ...), kind=kOutput, calls=%fused_computation.23 | convolution fusion | flops 809827328 | bytes 8009216 | tf_op jit(solution)/shard_map/dot_general | solution.py:176
  72.4 1.3 %fusion.48 = f32[256,4096]{1,0:T(8,128)S(1)} fusion(bf16[256,384]{1,0:T(8,128)(2,1)S(1)} %get-tuple-element.19, bf16[384,4096]{1,0:T(8,128)(2,1)S(1)} %bitcast.41), kind=kOutput, calls=%fused_computation.106 | convolution fusion | flops 805306368 | bytes 7536640 | tf_op jit(solution)/shard_map/dot_general | solution.py:203
  73.6 1.5 %fusion.2 = bf16[256,4096]{1,0:T(8,128)(2,1)S(1)} fusion(f32[256,4096]{1,0:T(8,128)S(1)} %fusion.48, bf16[384,4096]{1,0:T(8,128)(2,1)S(1)} %bitcast.44, f32[256,384]{1,0:T(8,128)S(1)} %fusion.45, f32[256]{0:T(256)S(1)} %get-tuple-element.16, f32[256]{0:T(256)S(1)} %get-tuple-element.15, s32[384]{0:T(512)S(1)} %add_select_fusion, ...), kind=kOutput, calls=%fused_computation.7 | convolution fusion | flops 808583168 | bytes 10229248 | tf_op jit(solution)/shard_map/dot_general | solution.py:204
  75.2 0.5 collective-permute-start.18
  75.7 1.3 %fusion.44 = f32[256,4096]{1,0:T(8,128)S(1)} fusion(bf16[256,384]{1,0:T(8,128)(2,1)S(1)} %get-tuple-element.20, bf16[384,4096]{1,0:T(8,128)(2,1)S(1)} %bitcast.39), kind=kOutput, calls=%fused_computation.102 | convolution fusion | flops 805306368 | bytes 7536640 | tf_op jit(solution)/shard_map/dot_general | solution.py:203
  77.0 1.4 %fusion.17 = f32[384,4096]{1,0:T(8,128)S(1)} fusion(bf16[256,4096]{1,0:T(8,128)(2,1)S(1)} %collective-permute-done.11, f32[256]{0:T(256)S(1)} %get-tuple-element.16, f32[256]{0:T(256)S(1)} %get-tuple-element.15, s32[384]{0:T(512)S(1)} %add_select_fusion, s32[256]{0:T(256)S(1)} %get-tuple-element.14, s32[256]{0:T(256)S(1)} %get-tuple-element.13, ...), kind=kOutput, calls=%fused_computation.45 | convolution fusion | flops 806486016 | bytes 9180672 | tf_op jit(solution)/shard_map/dot_general | solution.py:212
  78.4 2.9 %add_convert_fusion = bf16[384,4096]{1,0:T(8,128)(2,1)} fusion(f32[384,4096]{1,0:T(8,128)S(1)} %fusion.17, bf16[256,4096]{1,0:T(8,128)(2,1)S(1)} %constant_dynamic-update-slice_fusion.3, f32[256]{0:T(256)S(1)} %get-tuple-element.12, f32[256]{0:T(256)S(1)} %get-tuple-element.11, s32[384]{0:T(512)S(1)} %add_select_fusion, s32[256]{0:T(256)S(1)} %get-tuple-element.10, ...), kind=kOutput, calls=%fused_computation | convolution fusion | flops 809631744 | bytes 12326400 | tf_op jit(solution)/shard_map/dot_general | solution.py:212
  81.3 1.4 %add_convert_fusion.3 = bf16[256,4096]{1,0:T(8,128)(2,1)S(1)} fusion(bf16[256,4096]{1,0:T(8,128)(2,1)S(1)} %collective-permute-done.13, f32[256,4096]{1,0:T(8,128)S(1)} %fusion.44, bf16[384,4096]{1,0:T(8,128)(2,1)S(1)} %bitcast.45, f32[256,384]{1,0:T(8,128)S(1)} %get-tuple-element.27, f32[256]{0:T(256)S(1)} %get-tuple-element.12, ...), kind=kOutput, calls=%fused_computation.8 | convolution fusion | flops 812777472 | bytes 12326400 | tf_op jit(solution)/shard_map/dot_general | solution.py:204
  82.9 1.4 %collective-permute-start.14 = (bf16[128,4096]{1,0:T(8,128)(2,1)S(1)}, bf16[128,4096]{1,0:T(8,128)(2,1)S(1)}, u32[]{:S(2)}, u32[]{:S(2)}) collective-permute-start(bf16[128,4096]{1,0:T(8,128)(2,1)S(1)} %split.65), channel_id=1, source_target_pairs={{0,16},{1,9},{2,18},{3,11},{4,20},{5,13},{6,22},{7,15},{8,24},{9,1... | collective-permute-start | bytes 3145736 | tf_op jit(solution)/shard_map/ppermute | solution.py:109
  84.3 1.2 fusion.41
  85.6 0.7 collective-permute-start.19
  86.3 2.9 %add_convert_fusion.1 = bf16[384,4096]{1,0:T(8,128)(2,1)} fusion(f32[384,4096]{1,0:T(8,128)S(1)} %fusion.41, bf16[256,4096]{1,0:T(8,128)(2,1)S(1)} %pad_maximum_fusion, f32[256,384]{1,0:T(8,128)S(1)} %get-tuple-element.27, f32[256]{0:T(256)S(1)} %get-tuple-element.12, f32[256]{0:T(256)S(1)} %get-tuple-element.11, s32[384]{0:T(512)S(1)} %add_select_fusion, ...), kind=kOutput, calls=%fused_computation.1 | convolution fusion | flops 809631744 | bytes 12326400 | tf_op jit(solution)/shard_map/dot_general | solution.py:212
  89.2 8.6 %collective-permute-done.19 = f32[2,128]{1,0:T(2,128)S(1)} collective-permute-done((f32[2,128]{1,0:T(2,128)S(1)}, f32[2,128]{1,0:T(2,128)S(1)}, u32[]{:S(2)}, u32[]{:S(2)}) %collective-permute-start.19) | collective-permute-done | bytes 1056 | tf_op jit(solution)/shard_map/ppermute | solution.py:109
  97.8 1.5 %collective-permute-start.20 = (f32[2,64]{1,0:T(2,128)S(1)}, f32[2,64]{1,0:T(2,128)S(1)}, u32[]{:S(2)}, u32[]{:S(2)}) collective-permute-start(f32[2,64]{1,0:T(2,128)S(1)} %split.59), channel_id=1, source_target_pairs={{0,8},{1,17},{2,10},{3,19},{4,12},{5,21},{6,14},{7,23},{8,0},{9,25... | collective-permute-start | bytes 1544 | tf_op jit(solution)/shard_map/ppermute | solution.py:109
  99.3 0.2 add_convert_fusion.4
  99.6 0.6 collective-permute-start.15
  100.2 1.0 fusion.49
  101.2 0.2 collective-permute-done.20
  101.5 2.0 %collective-permute-start.21 = (f32[2,32]{1,0:T(2,128)S(1)}, f32[2,32]{1,0:T(2,128)S(1)}, u32[]{:S(2)}, u32[]{:S(2)}) collective-permute-start(f32[2,32]{1,0:T(2,128)S(1)} %split.61), channel_id=1, source_target_pairs={{0,2},{1,3},{2,0},{3,1},{4,6},{5,7},{6,4},{7,5},{8,10},{9,11},{10,... | collective-permute-start | bytes 776 | tf_op jit(solution)/shard_map/ppermute | solution.py:109
  103.5 5.3 %collective-permute-done.15 = bf16[64,4096]{1,0:T(8,128)(2,1)S(1)} collective-permute-done((bf16[64,4096]{1,0:T(8,128)(2,1)S(1)}, bf16[64,4096]{1,0:T(8,128)(2,1)S(1)}, u32[]{:S(2)}, u32[]{:S(2)}) %collective-permute-start.15) | collective-permute-done | bytes 524320 | tf_op jit(solution)/shard_map/ppermute | solution.py:109
  109.0 2.1 %collective-permute-start.16 = (bf16[32,4096]{1,0:T(8,128)(2,1)S(1)}, bf16[32,4096]{1,0:T(8,128)(2,1)S(1)}, u32[]{:S(2)}, u32[]{:S(2)}) collective-permute-start(bf16[32,4096]{1,0:T(8,128)(2,1)S(1)} %split.69), channel_id=1, source_target_pairs={{0,2},{1,3},{2,0},{3,1},{4,6},{5,7},{6,4},{7,5},{8,10},{9,11},{10,... | collective-permute-start | bytes 786440 | tf_op jit(solution)/shard_map/ppermute | solution.py:109
  111.1 2.8 %add_convert_fusion.2 = bf16[384,4096]{1,0:T(8,128)(2,1)} fusion(f32[384,4096]{1,0:T(8,128)S(1)} %fusion.49, bf16[256,384]{1,0:T(8,128)(2,1)S(1)} %get-tuple-element.20, bf16[256,4096]{1,0:T(8,128)(2,1)S(1)} %pad_maximum_fusion), kind=kOutput, calls=%fused_computation.2 | convolution fusion | flops 808452096 | bytes 11730944 | tf_op jit(solution)/shard_map/dot_general | solution.py:212
  114.0 3.3 %collective-permute-start.22 = (f32[2,16]{1,0:T(2,128)S(1)}, f32[2,16]{1,0:T(2,128)S(1)}, u32[]{:S(2)}, u32[]{:S(2)}) collective-permute-start(f32[2,16]{1,0:T(2,128)S(1)} %split.63), channel_id=1, source_target_pairs={{0,4},{1,5},{2,6},{3,7},{4,0},{5,1},{6,2},{7,3},{8,12},{9,13},{10,... | collective-permute-start | bytes 392 | tf_op jit(solution)/shard_map/ppermute | solution.py:109
  117.4 2.4 %collective-permute-start.17 = (bf16[16,4096]{1,0:T(8,128)(2,1)S(1)}, bf16[16,4096]{1,0:T(8,128)(2,1)S(1)}, u32[]{:S(2)}, u32[]{:S(2)}) collective-permute-start(bf16[16,4096]{1,0:T(8,128)(2,1)S(1)} %split.71), channel_id=1, source_target_pairs={{0,4},{1,5},{2,6},{3,7},{4,0},{5,1},{6,2},{7,3},{8,12},{9,13},{10,... | collective-permute-start | bytes 393224 | tf_op jit(solution)/shard_map/ppermute | solution.py:109
  119.8 0.6 add_bitcast_fusion
  120.4 4.3 %collective-permute-done.17 = bf16[16,4096]{1,0:T(8,128)(2,1)S(1)} collective-permute-done((bf16[16,4096]{1,0:T(8,128)(2,1)S(1)}, bf16[16,4096]{1,0:T(8,128)(2,1)S(1)}, u32[]{:S(2)}, u32[]{:S(2)}) %collective-permute-start.17) | collective-permute-done | bytes 131104 | tf_op jit(solution)/shard_map/ppermute | solution.py:109
  124.7 0.7 add_convert_fusion.7
  (61 shorter events, 1.7 us)
Async XLA Ops:
  0.6 62.1 %copy-start = (bf16[2,192,4096]{2,1,0:T(8,128)(2,1)S(1)}, bf16[2,192,4096]{2,1,0:T(8,128)(2,1)}, u32[]{:S(2)}) copy-start(bf16[2,192,4096]{2,1,0:T(8,128)(2,1)} %param.11) | copy-start | bytes 9437188
  0.6 27.8 %copy-start.4 = (bf16[16,4096]{1,0:T(8,128)(2,1)S(1)}, bf16[16,4096]{1,0:T(8,128)(2,1)}, u32[]{:S(2)}) copy-start(bf16[16,4096]{1,0:T(8,128)(2,1)} %param.7) | copy-start | bytes 393220
  0.7 10.8 %collective-permute-start.5 = (bf16[16,4096]{1,0:T(8,128)(2,1)}, bf16[16,4096]{1,0:T(8,128)(2,1)S(1)}, u32[]{:S(2)}, u32[]{:S(2)}) collective-permute-start(bf16[16,4096]{1,0:T(8,128)(2,1)} %param.8), channel_id=1, source_target_pairs={{0,4},{1,5},{2,6},{3,7},{4,0},{5,1},{6,2},{7,3},{8,12},{9,13},{10,... | collective-permute-start | bytes 393224 | tf_op jit(solution)/shard_map/ppermute | solution.py:109
  7.8 9.3 %collective-permute-start = (bf16[16,4224]{1,0:T(8,128)(2,1)}, bf16[16,4224]{1,0:T(8,128)(2,1)S(1)}, u32[]{:S(2)}, u32[]{:S(2)}) collective-permute-start(bf16[16,4224]{1,0:T(8,128)(2,1)} %pad_maximum_fusion.4), channel_id=1, source_target_pairs={{0,4},{1,5},{2,6},{3,7},{4,0},{5,1},{6,2},{7,3},{8,12},{9,13},{10,... | collective-permute-start | bytes 405512 | tf_op jit(solution)/shard_map/ppermute | solution.py:109
  12.4 10.8 %collective-permute-start.6 = (bf16[32,4096]{1,0:T(8,128)(2,1)S(1)}, bf16[32,4096]{1,0:T(8,128)(2,1)S(1)}, u32[]{:S(2)}, u32[]{:S(2)}) collective-permute-start(bf16[32,4096]{1,0:T(8,128)(2,1)S(1)} %pad_maximum_fusion.3), channel_id=1, source_target_pairs={{0,2},{1,3},{2,0},{3,1},{4,6},{5,7},{6,4},{7,5},{8,10},{9,11},{10,... | collective-permute-start | bytes 786440 | tf_op jit(solution)/shard_map/ppermute | solution.py:109
  18.0 10.5 %collective-permute-start.1 = (bf16[32,4224]{1,0:T(8,128)(2,1)S(1)}, bf16[32,4224]{1,0:T(8,128)(2,1)S(1)}, u32[]{:S(2)}, u32[]{:S(2)}) collective-permute-start(bf16[32,4224]{1,0:T(8,128)(2,1)S(1)} %pad_maximum_fusion.2), channel_id=1, source_target_pairs={{0,2},{1,3},{2,0},{3,1},{4,6},{5,7},{6,4},{7,5},{8,10},{9,11},{10,... | collective-permute-start | bytes 811016 | tf_op jit(solution)/shard_map/ppermute | solution.py:109
  24.0 17.1 %copy-start.3 = (bf16[256,4096]{1,0:T(8,128)(2,1)S(1)}, bf16[256,4096]{1,0:T(8,128)(2,1)}, u32[]{:S(2)}) copy-start(bf16[256,4096]{1,0:T(8,128)(2,1)} %get-tuple-element.22) | copy-start | bytes 6291460
  24.0 28.7 %collective-permute-start.8 = (bf16[64,4096]{1,0:T(8,128)(2,1)}, bf16[64,4096]{1,0:T(8,128)(2,1)S(1)}, u32[]{:S(2)}, u32[]{:S(2)}) collective-permute-start(bf16[64,4096]{1,0:T(8,128)(2,1)} %get-tuple-element.21), channel_id=1, source_target_pairs={{0,16},{1,9},{2,18},{3,11},{4,20},{5,13},{6,22},{7,15},{8,24},{9,1... | collective-permute-start | bytes 1572872 | tf_op jit(solution)/shard_map/ppermute | solution.py:109
  25.6 15.1 %collective-permute-start.7 = (bf16[64,4096]{1,0:T(8,128)(2,1)}, bf16[64,4096]{1,0:T(8,128)(2,1)S(1)}, u32[]{:S(2)}, u32[]{:S(2)}) collective-permute-start(bf16[64,4096]{1,0:T(8,128)(2,1)} %get-tuple-element.21), channel_id=1, source_target_pairs={{0,8},{1,17},{2,10},{3,19},{4,12},{5,21},{6,14},{7,23},{8,0},{9,25... | collective-permute-start | bytes 1572872 | tf_op jit(solution)/shard_map/ppermute | solution.py:109
  28.5 23.7 %collective-permute-start.2 = (bf16[64,4224]{1,0:T(8,128)(2,1)S(1)}, bf16[64,4224]{1,0:T(8,128)(2,1)S(1)}, u32[]{:S(2)}, u32[]{:S(2)}) collective-permute-start(bf16[64,4224]{1,0:T(8,128)(2,1)S(1)} %pad_maximum_fusion.1), channel_id=1, source_target_pairs={{0,8},{1,17},{2,10},{3,19},{4,12},{5,21},{6,14},{7,23},{8,0},{9,25... | collective-permute-start | bytes 1622024 | tf_op jit(solution)/shard_map/ppermute | solution.py:109
  30.2 22.6 %collective-permute-start.3 = (bf16[64,4224]{1,0:T(8,128)(2,1)S(1)}, bf16[64,4224]{1,0:T(8,128)(2,1)S(1)}, u32[]{:S(2)}, u32[]{:S(2)}) collective-permute-start(bf16[64,4224]{1,0:T(8,128)(2,1)S(1)} %pad_maximum_fusion.1), channel_id=1, source_target_pairs={{0,16},{1,9},{2,18},{3,11},{4,20},{5,13},{6,22},{7,15},{8,24},{9,1... | collective-permute-start | bytes 1622024 | tf_op jit(solution)/shard_map/ppermute | solution.py:109
  40.6 15.0 %collective-permute-start.9 = (bf16[64,4096]{1,0:T(8,128)(2,1)S(1)}, bf16[64,4096]{1,0:T(8,128)(2,1)S(1)}, u32[]{:S(2)}, u32[]{:S(2)}) collective-permute-start(bf16[64,4096]{1,0:T(8,128)(2,1)S(1)} %collective-permute-done.7), channel_id=1, source_target_pairs={{0,16},{1,9},{2,18},{3,11},{4,20},{5,13},{6,22},{7,15},{8,24},{9,1... | collective-permute-start | bytes 1572872 | tf_op jit(solution)/shard_map/ppermute | solution.py:109
  52.2 9.4 %collective-permute-start.4 = (bf16[64,4224]{1,0:T(8,128)(2,1)S(1)}, bf16[64,4224]{1,0:T(8,128)(2,1)S(1)}, u32[]{:S(2)}, u32[]{:S(2)}) collective-permute-start(bf16[64,4224]{1,0:T(8,128)(2,1)S(1)} %collective-permute-done.2), channel_id=1, source_target_pairs={{0,16},{1,9},{2,18},{3,11},{4,20},{5,13},{6,22},{7,15},{8,24},{9,1... | collective-permute-start | bytes 1622024 | tf_op jit(solution)/shard_map/ppermute | solution.py:109
  55.7 11.0 %collective-permute-start.11 = (bf16[256,4096]{1,0:T(8,128)(2,1)S(1)}, bf16[256,4096]{1,0:T(8,128)(2,1)S(1)}, u32[]{:S(2)}, u32[]{:S(2)}) collective-permute-start(bf16[256,4096]{1,0:T(8,128)(2,1)S(1)} %constant_dynamic-update-slice_fusion.3), channel_id=1, source_target_pairs={{0,1},{1,0},{2,3},{3,2},{4,5},{5,4},{6,7},{7,6},{8,9},{9,8},{10,11... | collective-permute-start | bytes 6291464 | tf_op jit(solution)/shard_map/ppermute | solution.py:109
  61.6 4.5 %collective-permute-start.10 = (bf16[256,128]{1,0:T(8,128)(2,1)S(1)}, bf16[256,128]{1,0:T(8,128)(2,1)S(1)}, u32[]{:S(2)}, u32[]{:S(2)}) collective-permute-start(bf16[256,128]{1,0:T(8,128)(2,1)S(1)} %pad_maximum_fusion.5), channel_id=1, source_target_pairs={{0,1},{1,0},{2,3},{3,2},{4,5},{5,4},{6,7},{7,6},{8,9},{9,8},{10,11... | collective-permute-start | bytes 196616 | tf_op jit(solution)/shard_map/ppermute | solution.py:109
  61.9 6.1 %collective-permute-start.12 = (bf16[256,4096]{1,0:T(8,128)(2,1)S(1)}, bf16[256,4096]{1,0:T(8,128)(2,1)S(1)}, u32[]{:S(2)}, u32[]{:S(2)}) collective-permute-start(bf16[256,4096]{1,0:T(8,128)(2,1)S(1)} %pad_maximum_fusion), channel_id=1, source_target_pairs={{0,1},{1,0},{2,3},{3,2},{4,5},{5,4},{6,7},{7,6},{8,9},{9,8},{10,11... | collective-permute-start | bytes 6291464 | tf_op jit(solution)/shard_map/ppermute | solution.py:109
  62.8 1.9 %copy-start.2 = (bf16[2,192,4096]{2,1,0:T(8,128)(2,1)S(1)}, bf16[2,192,4096]{2,1,0:T(8,128)(2,1)}, u32[]{:S(2)}) copy-start(bf16[2,192,4096]{2,1,0:T(8,128)(2,1)} %param.12) | copy-start | bytes 9437188
  64.7 2.0 %copy-start.5 = (bf16[2,192,4096]{2,1,0:T(8,128)(2,1)S(1)}, bf16[2,192,4096]{2,1,0:T(8,128)(2,1)}, u32[]{:S(2)}) copy-start(bf16[2,192,4096]{2,1,0:T(8,128)(2,1)} %param.13) | copy-start | bytes 9437188
  75.1 6.2 %collective-permute-start.13 = (bf16[256,4096]{1,0:T(8,128)(2,1)S(1)}, bf16[256,4096]{1,0:T(8,128)(2,1)S(1)}, u32[]{:S(2)}, u32[]{:S(2)}) collective-permute-start(bf16[256,4096]{1,0:T(8,128)(2,1)S(1)} %fusion.2), channel_id=1, source_target_pairs={{0,1},{1,0},{2,3},{3,2},{4,5},{5,4},{6,7},{7,6},{8,9},{9,8},{10,11... | collective-permute-start | bytes 6291464 | tf_op jit(solution)/shard_map/ppermute | solution.py:109
  75.2 10.3 %collective-permute-start.18 = (f32[2,256]{1,0:T(2,128)S(1)}, f32[2,256]{1,0:T(2,128)S(1)}, u32[]{:S(2)}, u32[]{:S(2)}) collective-permute-start(f32[2,256]{1,0:T(2,128)S(1)} %pad_maximum_fusion.6), channel_id=1, source_target_pairs={{0,1},{1,0},{2,3},{3,2},{4,5},{5,4},{6,7},{7,6},{8,9},{9,8},{10,11... | collective-permute-start | bytes 6152 | tf_op jit(solution)/shard_map/ppermute | solution.py:109
  82.9 16.5 %collective-permute-start.14 = (bf16[128,4096]{1,0:T(8,128)(2,1)S(1)}, bf16[128,4096]{1,0:T(8,128)(2,1)S(1)}, u32[]{:S(2)}, u32[]{:S(2)}) collective-permute-start(bf16[128,4096]{1,0:T(8,128)(2,1)S(1)} %split.65), channel_id=1, source_target_pairs={{0,16},{1,9},{2,18},{3,11},{4,20},{5,13},{6,22},{7,15},{8,24},{9,1... | collective-permute-start | bytes 3145736 | tf_op jit(solution)/shard_map/ppermute | solution.py:109
  85.6 12.2 %collective-permute-start.19 = (f32[2,128]{1,0:T(2,128)S(1)}, f32[2,128]{1,0:T(2,128)S(1)}, u32[]{:S(2)}, u32[]{:S(2)}) collective-permute-start(f32[2,128]{1,0:T(2,128)S(1)} %split.73), channel_id=1, source_target_pairs={{0,16},{1,9},{2,18},{3,11},{4,20},{5,13},{6,22},{7,15},{8,24},{9,1... | collective-permute-start | bytes 3080 | tf_op jit(solution)/shard_map/ppermute | solution.py:109
  97.8 3.6 %collective-permute-start.20 = (f32[2,64]{1,0:T(2,128)S(1)}, f32[2,64]{1,0:T(2,128)S(1)}, u32[]{:S(2)}, u32[]{:S(2)}) collective-permute-start(f32[2,64]{1,0:T(2,128)S(1)} %split.59), channel_id=1, source_target_pairs={{0,8},{1,17},{2,10},{3,19},{4,12},{5,21},{6,14},{7,23},{8,0},{9,25... | collective-permute-start | bytes 1544 | tf_op jit(solution)/shard_map/ppermute | solution.py:109
  99.6 9.2 %collective-permute-start.15 = (bf16[64,4096]{1,0:T(8,128)(2,1)S(1)}, bf16[64,4096]{1,0:T(8,128)(2,1)S(1)}, u32[]{:S(2)}, u32[]{:S(2)}) collective-permute-start(bf16[64,4096]{1,0:T(8,128)(2,1)S(1)} %split.67), channel_id=1, source_target_pairs={{0,8},{1,17},{2,10},{3,19},{4,12},{5,21},{6,14},{7,23},{8,0},{9,25... | collective-permute-start | bytes 1572872 | tf_op jit(solution)/shard_map/ppermute | solution.py:109
  101.5 12.4 %collective-permute-start.21 = (f32[2,32]{1,0:T(2,128)S(1)}, f32[2,32]{1,0:T(2,128)S(1)}, u32[]{:S(2)}, u32[]{:S(2)}) collective-permute-start(f32[2,32]{1,0:T(2,128)S(1)} %split.61), channel_id=1, source_target_pairs={{0,2},{1,3},{2,0},{3,1},{4,6},{5,7},{6,4},{7,5},{8,10},{9,11},{10,... | collective-permute-start | bytes 776 | tf_op jit(solution)/shard_map/ppermute | solution.py:109
  109.0 8.3 %collective-permute-start.16 = (bf16[32,4096]{1,0:T(8,128)(2,1)S(1)}, bf16[32,4096]{1,0:T(8,128)(2,1)S(1)}, u32[]{:S(2)}, u32[]{:S(2)}) collective-permute-start(bf16[32,4096]{1,0:T(8,128)(2,1)S(1)} %split.69), channel_id=1, source_target_pairs={{0,2},{1,3},{2,0},{3,1},{4,6},{5,7},{6,4},{7,5},{8,10},{9,11},{10,... | collective-permute-start | bytes 786440 | tf_op jit(solution)/shard_map/ppermute | solution.py:109
  111.1 14.3 %copy-start.1 = (bf16[2,192,4096]{2,1,0:T(8,128)(2,1)S(1)}, bf16[2,192,4096]{2,1,0:T(8,128)(2,1)}, u32[]{:S(2)}) copy-start(bf16[2,192,4096]{2,1,0:T(8,128)(2,1)} %param.11) | copy-start | bytes 9437188
  114.0 5.8 %collective-permute-start.22 = (f32[2,16]{1,0:T(2,128)S(1)}, f32[2,16]{1,0:T(2,128)S(1)}, u32[]{:S(2)}, u32[]{:S(2)}) collective-permute-start(f32[2,16]{1,0:T(2,128)S(1)} %split.63), channel_id=1, source_target_pairs={{0,4},{1,5},{2,6},{3,7},{4,0},{5,1},{6,2},{7,3},{8,12},{9,13},{10,... | collective-permute-start | bytes 392 | tf_op jit(solution)/shard_map/ppermute | solution.py:109
  117.4 7.3 %collective-permute-start.17 = (bf16[16,4096]{1,0:T(8,128)(2,1)S(1)}, bf16[16,4096]{1,0:T(8,128)(2,1)S(1)}, u32[]{:S(2)}, u32[]{:S(2)}) collective-permute-start(bf16[16,4096]{1,0:T(8,128)(2,1)S(1)} %split.71), channel_id=1, source_target_pairs={{0,4},{1,5},{2,6},{3,7},{4,0},{5,1},{6,2},{7,3},{8,12},{9,13},{10,... | collective-permute-start | bytes 393224 | tf_op jit(solution)/shard_map/ppermute | solution.py:109

commit v3 on v2

--- a/solution.py
+++ b/solution.py
@@ -121,6 +121,13 @@
     return along_dp, across
 
 
+def line_masks(along_dp):
+    masks = [0]
+    for step, _ in along_dp:
+        masks = masks + [mask ^ step for mask in masks]
+    return masks
+
+
 def collect(own, axis):
     along_dp, across = swap_order()
     block = own
@@ -132,16 +139,24 @@
     return pieces
 
 
-def hand_out(half, other, axis):
+def hand_out(half, other, axis, direct):
     along_dp, across = swap_order()
 
     def plus(kept, came):
         return (kept.astype(jnp.float32) + came.astype(jnp.float32)).astype(kept.dtype)
 
     half = plus(half, swap(other, (1, 1)))
-    for masks in across[::-1] + along_dp[::-1]:
+    for masks in across[::-1] + ([] if direct else along_dp[::-1]):
         kept, sent = jnp.split(half, 2, axis=axis)
         half = plus(kept, swap(sent, masks))
+    if direct:
+        masks = line_masks(along_dp)
+        pieces = jnp.split(half, len(masks), axis=axis)
+        total = sum(
+            (swap(piece, (m, m)) if m else piece).astype(jnp.float32)
+            for m, piece in zip(masks, pieces)
+        )
+        half = total.astype(half.dtype)
     return half
 
 
@@ -204,8 +219,8 @@
         input_part = input_part + jnp.dot(grad_up_pre, up_mat, preferred_element_type=jnp.float32)
         input_parts.append(input_part.astype(jnp.bfloat16))
         lefts.append((grad_gate_pre, grad_up_pre, weighted_hidden))
-    grad_tokens = hand_out(input_parts[0], input_parts[1], 0)
-    grad_gates = hand_out(gate_parts[0], gate_parts[1], 1).T
+    grad_tokens = hand_out(input_parts[0], input_parts[1], 0, True)
+    grad_gates = hand_out(gate_parts[0], gate_parts[1], 1, False).T
     weight_grads = []
     for left, right in ((0, xs), (1, xs), (2, dys)):
         total = sum(

time: 126 us -> 123 us (0.976)
  waiting for transfers between devices: 54.7 us -> 52.7 us
    ppermute x23 -> x24, waiting for transfers between devices: 54.7 us -> 52.7 us  [swap(): return lax.ppermute(values, ('expert', 'dp'), pairs)]
    ppermute x23 -> x24, starting transfers between devices: 31.5 us -> 31.5 us  [swap(): return lax.ppermute(values, ('expert', 'dp'), pairs)]
    unnamed x17 -> x15, local copies, waits for them, and re-layouts: 3.15 us -> 3.14 us
  transfers between devices with their start and end apart: 23 -> 24, of which waited for: 12 -> 13; matrix products, arithmetic and copies ran while one was open for 24% -> 24% of each run, Pallas kernels for 0% -> 0%
where the time goes in v3:
time: 123 us
  waiting for transfers between devices  52.7 us (43%)
  starting transfers between devices  31.5 us (26%)
  matrix products  25.5 us (21%)
  other arithmetic  6.92 us (6%)
  local copies, waits for them, and re-layouts  5.35 us (4%)
    ppermute x24, waiting for transfers between devices, swap(): return lax.ppermute(values, ('expert', 'dp'), pairs)  52.7 us
    ppermute x24, starting transfers between devices, swap(): return lax.ppermute(values, ('expert', 'dp'), pairs)  31.5 us
    dot_general x6, matrix products, all_tokens(): lax.dot_general(lefts[i][left], right[i], over_rows, preferred_element_ty...  12.1 us
    unnamed x15, local copies, waits for them, and re-layouts  3.14 us
    dot_general x2, matrix products, all_tokens(): lax.dot_general(dy, down_mat, over_width, preferred_element_type=jnp.floa...  3.07 us
    dot_general x2, matrix products, all_tokens(): jnp.dot(grad_up_pre, up_mat, preferred_element_type=jnp.float32)  2.79 us
    dot_general x2, matrix products, all_tokens(): lax.dot_general(x, up_mat, over_width, preferred_element_type=jnp.float32)  2.53 us
    dot_general x2, matrix products, all_tokens(): lax.dot_general(x, gate_mat, over_width, preferred_element_type=jnp.float32)  2.52 us
  transfers between devices with their start and end apart: 24, of which 13 were waited for; matrix products, arithmetic and copies ran while one was open for 24% of the time, Pallas kernels for 0%

profile of v3, /device:TPU:0, one launch (start us, length us, event | category | flops | bytes accessed | tf_op | source)
XLA Modules:
  0.0 123.0 jit_solution(11449411672080946010)
XLA Ops:
  0.7 4.1 %collective-permute-start.5 = (bf16[16,4096]{1,0:T(8,128)(2,1)}, bf16[16,4096]{1,0:T(8,128)(2,1)S(1)}, u32[]{:S(2)}, u32[]{:S(2)}) collective-permute-start(bf16[16,4096]{1,0:T(8,128)(2,1)} %param.8), channel_id=1, source_target_pairs={{0,4},{1,5},{2,6},{3,7},{4,0},{5,1},{6,2},{7,3},{8,12},{9,13},{10,... | collective-permute-start | bytes 393224 | tf_op jit(solution)/shard_map/ppermute | solution.py:109
  4.8 0.7 convert_element_type.92
  5.4 0.7 pad_maximum_fusion.7
  6.2 1.6 %pad_maximum_fusion.4 = bf16[16,4224]{1,0:T(8,128)(2,1)} fusion(bf16[16,128]{1,0:T(8,128)(2,1)S(1)} %pad.4.clone, bf16[16,4096]{1,0:T(8,128)(2,1)} %param.7), kind=kLoop, calls=%fused_computation.57 | loop fusion | flops 270336 | bytes 270336 | tf_op jit(solution)/shard_map/concatenate | solution.py:169
  7.8 0.3 collective-permute-start
  8.0 1.6 %constant_dynamic-update-slice_fusion.2 = (bf16[64,4096]{1,0:T(8,128)(2,1)}, bf16[256,4096]{1,0:T(8,128)(2,1)}) fusion(bf16[16,4096]{1,0:T(8,128)(2,1)} %param.8), kind=kLoop, calls=%fused_computation.75 | loop fusion | bytes 393216
  9.7 1.8 %collective-permute-done.5 = bf16[16,4096]{1,0:T(8,128)(2,1)S(1)} collective-permute-done((bf16[16,4096]{1,0:T(8,128)(2,1)}, bf16[16,4096]{1,0:T(8,128)(2,1)S(1)}, u32[]{:S(2)}, u32[]{:S(2)}) %collective-permute-start.5) | collective-permute-done | bytes 131104 | tf_op jit(solution)/shard_map/ppermute | solution.py:109
  11.4 0.9 pad_maximum_fusion.3
  12.4 3.7 %collective-permute-start.6 = (bf16[32,4096]{1,0:T(8,128)(2,1)S(1)}, bf16[32,4096]{1,0:T(8,128)(2,1)S(1)}, u32[]{:S(2)}, u32[]{:S(2)}) collective-permute-start(bf16[32,4096]{1,0:T(8,128)(2,1)S(1)} %pad_maximum_fusion.3), channel_id=1, source_target_pairs={{0,2},{1,3},{2,0},{3,1},{4,6},{5,7},{6,4},{7,5},{8,10},{9,11},{10,... | collective-permute-start | bytes 786440 | tf_op jit(solution)/shard_map/ppermute | solution.py:109
  16.1 0.7 constant_dynamic-update-slice_fusion.1
  16.8 0.3 collective-permute-done
  17.1 0.9 pad_maximum_fusion.2
  18.0 0.9 collective-permute-start.1
  18.9 4.3 %collective-permute-done.6 = bf16[32,4096]{1,0:T(8,128)(2,1)S(1)} collective-permute-done((bf16[32,4096]{1,0:T(8,128)(2,1)S(1)}, bf16[32,4096]{1,0:T(8,128)(2,1)S(1)}, u32[]{:S(2)}, u32[]{:S(2)}) %collective-permute-start.6) | collective-permute-done | bytes 262176 | tf_op jit(solution)/shard_map/ppermute | solution.py:109
  23.2 0.8 constant_dynamic-update-slice_fusion
  24.0 1.5 %collective-permute-start.8 = (bf16[64,4096]{1,0:T(8,128)(2,1)}, bf16[64,4096]{1,0:T(8,128)(2,1)S(1)}, u32[]{:S(2)}, u32[]{:S(2)}) collective-permute-start(bf16[64,4096]{1,0:T(8,128)(2,1)} %get-tuple-element.24), channel_id=1, source_target_pairs={{0,16},{1,9},{2,18},{3,11},{4,20},{5,13},{6,22},{7,15},{8,24},{9,1... | collective-permute-start | bytes 1572872 | tf_op jit(solution)/shard_map/ppermute | solution.py:109
  25.6 1.5 %collective-permute-start.7 = (bf16[64,4096]{1,0:T(8,128)(2,1)}, bf16[64,4096]{1,0:T(8,128)(2,1)S(1)}, u32[]{:S(2)}, u32[]{:S(2)}) collective-permute-start(bf16[64,4096]{1,0:T(8,128)(2,1)} %get-tuple-element.24), channel_id=1, source_target_pairs={{0,8},{1,17},{2,10},{3,19},{4,12},{5,21},{6,14},{7,23},{8,0},{9,25... | collective-permute-start | bytes 1572872 | tf_op jit(solution)/shard_map/ppermute | solution.py:109
  27.0 1.4 %collective-permute-done.1 = bf16[32,4224]{1,0:T(8,128)(2,1)S(1)} collective-permute-done((bf16[32,4224]{1,0:T(8,128)(2,1)S(1)}, bf16[32,4224]{1,0:T(8,128)(2,1)S(1)}, u32[]{:S(2)}, u32[]{:S(2)}) %collective-permute-start.1) | collective-permute-done | bytes 270368 | tf_op jit(solution)/shard_map/ppermute | solution.py:109
  28.5 1.6 %collective-permute-start.2 = (bf16[64,4224]{1,0:T(8,128)(2,1)S(1)}, bf16[64,4224]{1,0:T(8,128)(2,1)S(1)}, u32[]{:S(2)}, u32[]{:S(2)}) collective-permute-start(bf16[64,4224]{1,0:T(8,128)(2,1)S(1)} %pad_maximum_fusion.1), channel_id=1, source_target_pairs={{0,8},{1,17},{2,10},{3,19},{4,12},{5,21},{6,14},{7,23},{8,0},{9,25... | collective-permute-start | bytes 1622024 | tf_op jit(solution)/shard_map/ppermute | solution.py:109
  30.2 1.6 %collective-permute-start.3 = (bf16[64,4224]{1,0:T(8,128)(2,1)S(1)}, bf16[64,4224]{1,0:T(8,128)(2,1)S(1)}, u32[]{:S(2)}, u32[]{:S(2)}) collective-permute-start(bf16[64,4224]{1,0:T(8,128)(2,1)S(1)} %pad_maximum_fusion.1), channel_id=1, source_target_pairs={{0,16},{1,9},{2,18},{3,11},{4,20},{5,13},{6,22},{7,15},{8,24},{9,1... | collective-permute-start | bytes 1622024 | tf_op jit(solution)/shard_map/ppermute | solution.py:109
  31.8 8.9 %collective-permute-done.7 = bf16[64,4096]{1,0:T(8,128)(2,1)S(1)} collective-permute-done((bf16[64,4096]{1,0:T(8,128)(2,1)}, bf16[64,4096]{1,0:T(8,128)(2,1)S(1)}, u32[]{:S(2)}, u32[]{:S(2)}) %collective-permute-start.7) | collective-permute-done | bytes 524320 | tf_op jit(solution)/shard_map/ppermute | solution.py:109
  40.6 0.5 collective-permute-start.9
  41.2 11.0 %collective-permute-done.2 = bf16[64,4224]{1,0:T(8,128)(2,1)S(1)} collective-permute-done((bf16[64,4224]{1,0:T(8,128)(2,1)S(1)}, bf16[64,4224]{1,0:T(8,128)(2,1)S(1)}, u32[]{:S(2)}, u32[]{:S(2)}) %collective-permute-start.2) | collective-permute-done | bytes 540704 | tf_op jit(solution)/shard_map/ppermute | solution.py:109
  52.2 0.5 collective-permute-start.4
  52.9 2.8 %collective-permute-done.9 = bf16[64,4096]{1,0:T(8,128)(2,1)S(1)} collective-permute-done((bf16[64,4096]{1,0:T(8,128)(2,1)S(1)}, bf16[64,4096]{1,0:T(8,128)(2,1)S(1)}, u32[]{:S(2)}, u32[]{:S(2)}) %collective-permute-start.9) | collective-permute-done | bytes 524320 | tf_op jit(solution)/shard_map/ppermute | solution.py:109
  55.8 5.8 %collective-permute-done.4 = bf16[64,4224]{1,0:T(8,128)(2,1)S(1)} collective-permute-done((bf16[64,4224]{1,0:T(8,128)(2,1)S(1)}, bf16[64,4224]{1,0:T(8,128)(2,1)S(1)}, u32[]{:S(2)}, u32[]{:S(2)}) %collective-permute-start.4) | collective-permute-done | bytes 540704 | tf_op jit(solution)/shard_map/ppermute | solution.py:109
  61.9 0.6 collective-permute-start.12
  62.6 0.2 slice_reduce_fusion.7
  62.8 1.3 %fusion.44 = f32[256,384]{1,0:T(8,128)S(1)} fusion(bf16[256,4096]{1,0:T(8,128)(2,1)S(1)} %pad_maximum_fusion, bf16[384,4096]{1,0:T(8,128)(2,1)S(1)} %bitcast.38), kind=kOutput, calls=%fused_computation.101 | convolution fusion | flops 805306368 | bytes 5636096 | tf_op jit(solution)/shard_map/dot_general | solution.py:189
  64.1 0.6 copy-done.1
  64.7 1.3 %fusion.43 = f32[256,384]{1,0:T(8,128)S(1)} fusion(bf16[256,4096]{1,0:T(8,128)(2,1)S(1)} %pad_maximum_fusion, bf16[384,4096]{1,0:T(8,128)(2,1)S(1)} %bitcast.42), kind=kOutput, calls=%fused_computation.100 | convolution fusion | flops 805306368 | bytes 5636096 | tf_op jit(solution)/shard_map/dot_general | solution.py:190
  66.0 0.2 slice_reduce_fusion.6
  66.2 0.2 slice_reduce_fusion.2
  66.7 1.3 %fusion.46 = f32[256,384]{1,0:T(8,128)S(1)} fusion(bf16[256,4096]{1,0:T(8,128)(2,1)S(1)} %collective-permute-done.11, bf16[384,4096]{1,0:T(8,128)(2,1)S(1)} %bitcast.53), kind=kOutput, calls=%fused_computation.103 | convolution fusion | flops 805306368 | bytes 5636096 | tf_op jit(solution)/shard_map/dot_general | solution.py:191
  68.0 1.3 %fusion.48 = f32[256,384]{1,0:T(8,128)S(1)} fusion(bf16[256,4096]{1,0:T(8,128)(2,1)S(1)} %collective-permute-done.12, bf16[384,4096]{1,0:T(8,128)(2,1)S(1)} %bitcast.40), kind=kOutput, calls=%fused_computation.105 | convolution fusion | flops 805306368 | bytes 5636096 | tf_op jit(solution)/shard_map/dot_general | solution.py:189
  69.3 1.3 %fusion.47 = f32[256,384]{1,0:T(8,128)S(1)} fusion(bf16[256,4096]{1,0:T(8,128)(2,1)S(1)} %collective-permute-done.12, bf16[384,4096]{1,0:T(8,128)(2,1)S(1)} %bitcast.43), kind=kOutput, calls=%fused_computation.104 | convolution fusion | flops 805306368 | bytes 5636096 | tf_op jit(solution)/shard_map/dot_general | solution.py:190
  70.6 1.8 %fusion.4 = (f32[256]{0:T(256)S(1)}, f32[256]{0:T(256)S(1)}, f32[256]{0:T(256)S(1)}, f32[256]{0:T(256)S(1)}, bf16[256,384]{1,0:T(8,128)(2,1)S(1)}, /*index=5*/bf16[256,384]{1,0:T(8,128)(2,1)S(1)}, f32[256,384]{1,0:T(8,128)S(1)}) fusion(s32[384]{0:T(512)S(1)} %add_select_fusion, s32[256]{0:T(256)S(1)} %get-tuple-element.9, f32[256,384]{1,0:T(8,128)S(1)} %fusion.43, ...), kind=kOutput, calls=%fused_computation.22 | convolution fusion | flops 809827328 | bytes 8009216 | tf_op jit(solution)/shard_map/dot_general | solution.py:191
  72.4 1.3 %fusion.49 = f32[256,4096]{1,0:T(8,128)S(1)} fusion(bf16[256,384]{1,0:T(8,128)(2,1)S(1)} %get-tuple-element.19, bf16[384,4096]{1,0:T(8,128)(2,1)S(1)} %bitcast.41), kind=kOutput, calls=%fused_computation.106 | convolution fusion | flops 805306368 | bytes 7536640 | tf_op jit(solution)/shard_map/dot_general | solution.py:218
  73.6 1.4 %fusion.2 = bf16[256,4096]{1,0:T(8,128)(2,1)S(1)} fusion(f32[256,4096]{1,0:T(8,128)S(1)} %fusion.49, bf16[384,4096]{1,0:T(8,128)(2,1)S(1)} %bitcast.44, f32[256,384]{1,0:T(8,128)S(1)} %fusion.46, f32[256]{0:T(256)S(1)} %get-tuple-element.16, f32[256]{0:T(256)S(1)} %get-tuple-element.15, s32[384]{0:T(512)S(1)} %add_select_fusion, ...), kind=kOutput, calls=%fused_computation.7 | convolution fusion | flops 808583168 | bytes 10229248 | tf_op jit(solution)/shard_map/dot_general | solution.py:219
  75.1 0.5 collective-permute-start.19
  75.6 1.2 fusion.17
  76.8 1.4 %fusion.41 = f32[384,4096]{1,0:T(8,128)S(1)} fusion(bf16[256,4096]{1,0:T(8,128)(2,1)S(1)} %collective-permute-done.12, f32[256,384]{1,0:T(8,128)S(1)} %fusion.46, f32[256]{0:T(256)S(1)} %get-tuple-element.16, f32[256]{0:T(256)S(1)} %get-tuple-element.15, s32[384]{0:T(512)S(1)} %add_select_fusion, s32[256]{0:T(256)S(1)} %get-tuple-element.14, ...), kind=kOutput, calls=%fused_computation.98 | convolution fusion | flops 806486016 | bytes 9180672 | tf_op jit(solution)/shard_map/dot_general | solution.py:227
  78.2 2.9 %add_convert_fusion = bf16[384,4096]{1,0:T(8,128)(2,1)} fusion(f32[384,4096]{1,0:T(8,128)S(1)} %fusion.17, bf16[256,4096]{1,0:T(8,128)(2,1)S(1)} %constant_dynamic-update-slice_fusion.3, f32[256]{0:T(256)S(1)} %get-tuple-element.12, f32[256]{0:T(256)S(1)} %get-tuple-element.11, s32[384]{0:T(512)S(1)} %add_select_fusion, s32[256]{0:T(256)S(1)} %get-tuple-element.10, ...), kind=kOutput, calls=%fused_computation | convolution fusion | flops 809631744 | bytes 12326400 | tf_op jit(solution)/shard_map/dot_general | solution.py:227
  81.1 1.2 %fusion.45 = f32[256,4096]{1,0:T(8,128)S(1)} fusion(bf16[256,384]{1,0:T(8,128)(2,1)S(1)} %get-tuple-element.20, bf16[384,4096]{1,0:T(8,128)(2,1)S(1)} %bitcast.39), kind=kOutput, calls=%fused_computation.102 | convolution fusion | flops 805306368 | bytes 7536640 | tf_op jit(solution)/shard_map/dot_general | solution.py:218
  82.4 1.4 %collective-permute-start.20 = (f32[2,128]{1,0:T(2,128)S(1)}, f32[2,128]{1,0:T(2,128)S(1)}, u32[]{:S(2)}, u32[]{:S(2)}) collective-permute-start(f32[2,128]{1,0:T(2,128)S(1)} %split.73), channel_id=1, source_target_pairs={{0,16},{1,9},{2,18},{3,11},{4,20},{5,13},{6,22},{7,15},{8,24},{9,1... | collective-permute-start | bytes 3080 | tf_op jit(solution)/shard_map/ppermute | solution.py:109
  83.8 1.4 %add_convert_fusion.3 = bf16[256,4096]{1,0:T(8,128)(2,1)S(1)} fusion(bf16[256,4096]{1,0:T(8,128)(2,1)S(1)} %collective-permute-done.13, f32[256,4096]{1,0:T(8,128)S(1)} %fusion.45, bf16[384,4096]{1,0:T(8,128)(2,1)S(1)} %bitcast.45, f32[256,384]{1,0:T(8,128)S(1)} %get-tuple-element.30, f32[256]{0:T(256)S(1)} %get-tuple-element.12, ...), kind=kOutput, calls=%fused_computation.8 | convolution fusion | flops 812777472 | bytes 12326400 | tf_op jit(solution)/shard_map/dot_general | solution.py:219
  85.4 0.7 collective-permute-start.14
  86.1 2.9 %add_convert_fusion.1 = bf16[384,4096]{1,0:T(8,128)(2,1)} fusion(f32[384,4096]{1,0:T(8,128)S(1)} %fusion.41, bf16[256,4096]{1,0:T(8,128)(2,1)S(1)} %pad_maximum_fusion, f32[256,384]{1,0:T(8,128)S(1)} %get-tuple-element.30, f32[256]{0:T(256)S(1)} %get-tuple-element.12, f32[256]{0:T(256)S(1)} %get-tuple-element.11, s32[384]{0:T(512)S(1)} %add_select_fusion, ...), kind=kOutput, calls=%fused_computation.1 | convolution fusion | flops 809631744 | bytes 12326400 | tf_op jit(solution)/shard_map/dot_general | solution.py:227
  89.0 1.5 %collective-permute-start.21 = (f32[2,64]{1,0:T(2,128)S(1)}, f32[2,64]{1,0:T(2,128)S(1)}, u32[]{:S(2)}, u32[]{:S(2)}) collective-permute-start(f32[2,64]{1,0:T(2,128)S(1)} %split.59), channel_id=1, source_target_pairs={{0,8},{1,17},{2,10},{3,19},{4,12},{5,21},{6,14},{7,23},{8,0},{9,25... | collective-permute-start | bytes 1544 | tf_op jit(solution)/shard_map/ppermute | solution.py:109
  90.5 1.0 fusion.50
  91.5 1.2 collective-permute-done.21
  92.8 2.0 %collective-permute-start.22 = (f32[2,32]{1,0:T(2,128)S(1)}, f32[2,32]{1,0:T(2,128)S(1)}, u32[]{:S(2)}, u32[]{:S(2)}) collective-permute-start(f32[2,32]{1,0:T(2,128)S(1)} %split.61), channel_id=1, source_target_pairs={{0,2},{1,3},{2,0},{3,1},{4,6},{5,7},{6,4},{7,5},{8,10},{9,11},{10,... | collective-permute-start | bytes 776 | tf_op jit(solution)/shard_map/ppermute | solution.py:109
  94.8 5.4 %collective-permute-done.14 = bf16[128,4096]{1,0:T(8,128)(2,1)S(1)} collective-permute-done((bf16[128,4096]{1,0:T(8,128)(2,1)S(1)}, bf16[128,4096]{1,0:T(8,128)(2,1)S(1)}, u32[]{:S(2)}, u32[]{:S(2)}) %collective-permute-start.14) | collective-permute-done | bytes 1048608 | tf_op jit(solution)/shard_map/ppermute | solution.py:109
  100.2 0.2 add_convert_fusion.4
  100.5 0.7 collective-permute-start.15
  101.2 2.7 %add_convert_fusion.2 = bf16[384,4096]{1,0:T(8,128)(2,1)} fusion(f32[384,4096]{1,0:T(8,128)S(1)} %fusion.50, bf16[256,384]{1,0:T(8,128)(2,1)S(1)} %get-tuple-element.20, bf16[256,4096]{1,0:T(8,128)(2,1)S(1)} %pad_maximum_fusion), kind=kOutput, calls=%fused_computation.2 | convolution fusion | flops 808452096 | bytes 11730944 | tf_op jit(solution)/shard_map/dot_general | solution.py:227
  104.0 3.3 %collective-permute-start.23 = (f32[2,16]{1,0:T(2,128)S(1)}, f32[2,16]{1,0:T(2,128)S(1)}, u32[]{:S(2)}, u32[]{:S(2)}) collective-permute-start(f32[2,16]{1,0:T(2,128)S(1)} %split.63), channel_id=1, source_target_pairs={{0,4},{1,5},{2,6},{3,7},{4,0},{5,1},{6,2},{7,3},{8,12},{9,13},{10,... | collective-permute-start | bytes 392 | tf_op jit(solution)/shard_map/ppermute | solution.py:109
  107.2 2.5 %collective-permute-done.15 = bf16[64,4096]{1,0:T(8,128)(2,1)S(1)} collective-permute-done((bf16[64,4096]{1,0:T(8,128)(2,1)S(1)}, bf16[64,4096]{1,0:T(8,128)(2,1)S(1)}, u32[]{:S(2)}, u32[]{:S(2)}) %collective-permute-start.15) | collective-permute-done | bytes 524320 | tf_op jit(solution)/shard_map/ppermute | solution.py:109
  109.9 2.8 %collective-permute-start.16 = (bf16[16,4096]{1,0:T(8,128)(2,1)S(1)}, bf16[16,4096]{1,0:T(8,128)(2,1)S(1)}, u32[]{:S(2)}, u32[]{:S(2)}) collective-permute-start(bf16[16,4096]{1,0:T(8,128)(2,1)S(1)} %get-tuple-element.21), channel_id=1, source_target_pairs={{0,4},{1,5},{2,6},{3,7},{4,0},{5,1},{6,2},{7,3},{8,12},{9,13},{10,... | collective-permute-start | bytes 393224 | tf_op jit(solution)/shard_map/ppermute | solution.py:109
  112.8 1.2 collective-permute-start.18
  114.0 0.5 collective-permute-start.17
  114.5 0.6 add_bitcast_fusion
  115.0 7.1 %collective-permute-done.16 = bf16[16,4096]{1,0:T(8,128)(2,1)S(1)} collective-permute-done((bf16[16,4096]{1,0:T(8,128)(2,1)S(1)}, bf16[16,4096]{1,0:T(8,128)(2,1)S(1)}, u32[]{:S(2)}, u32[]{:S(2)}) %collective-permute-start.16) | collective-permute-done | bytes 131104 | tf_op jit(solution)/shard_map/ppermute | solution.py:109
  122.3 0.7 add_convert_fusion.6
  (59 shorter events, 1.9 us)
Async XLA Ops:
  0.6 62.2 %copy-start = (bf16[2,192,4096]{2,1,0:T(8,128)(2,1)S(1)}, bf16[2,192,4096]{2,1,0:T(8,128)(2,1)}, u32[]{:S(2)}) copy-start(bf16[2,192,4096]{2,1,0:T(8,128)(2,1)} %param.11) | copy-start | bytes 9437188
  0.6 27.8 %copy-start.3 = (bf16[16,4096]{1,0:T(8,128)(2,1)S(1)}, bf16[16,4096]{1,0:T(8,128)(2,1)}, u32[]{:S(2)}) copy-start(bf16[16,4096]{1,0:T(8,128)(2,1)} %param.7) | copy-start | bytes 393220
  0.7 10.8 %collective-permute-start.5 = (bf16[16,4096]{1,0:T(8,128)(2,1)}, bf16[16,4096]{1,0:T(8,128)(2,1)S(1)}, u32[]{:S(2)}, u32[]{:S(2)}) collective-permute-start(bf16[16,4096]{1,0:T(8,128)(2,1)} %param.8), channel_id=1, source_target_pairs={{0,4},{1,5},{2,6},{3,7},{4,0},{5,1},{6,2},{7,3},{8,12},{9,13},{10,... | collective-permute-start | bytes 393224 | tf_op jit(solution)/shard_map/ppermute | solution.py:109
  7.8 9.3 %collective-permute-start = (bf16[16,4224]{1,0:T(8,128)(2,1)}, bf16[16,4224]{1,0:T(8,128)(2,1)S(1)}, u32[]{:S(2)}, u32[]{:S(2)}) collective-permute-start(bf16[16,4224]{1,0:T(8,128)(2,1)} %pad_maximum_fusion.4), channel_id=1, source_target_pairs={{0,4},{1,5},{2,6},{3,7},{4,0},{5,1},{6,2},{7,3},{8,12},{9,13},{10,... | collective-permute-start | bytes 405512 | tf_op jit(solution)/shard_map/ppermute | solution.py:109
  12.4 10.8 %collective-permute-start.6 = (bf16[32,4096]{1,0:T(8,128)(2,1)S(1)}, bf16[32,4096]{1,0:T(8,128)(2,1)S(1)}, u32[]{:S(2)}, u32[]{:S(2)}) collective-permute-start(bf16[32,4096]{1,0:T(8,128)(2,1)S(1)} %pad_maximum_fusion.3), channel_id=1, source_target_pairs={{0,2},{1,3},{2,0},{3,1},{4,6},{5,7},{6,4},{7,5},{8,10},{9,11},{10,... | collective-permute-start | bytes 786440 | tf_op jit(solution)/shard_map/ppermute | solution.py:109
  18.0 10.5 %collective-permute-start.1 = (bf16[32,4224]{1,0:T(8,128)(2,1)S(1)}, bf16[32,4224]{1,0:T(8,128)(2,1)S(1)}, u32[]{:S(2)}, u32[]{:S(2)}) collective-permute-start(bf16[32,4224]{1,0:T(8,128)(2,1)S(1)} %pad_maximum_fusion.2), channel_id=1, source_target_pairs={{0,2},{1,3},{2,0},{3,1},{4,6},{5,7},{6,4},{7,5},{8,10},{9,11},{10,... | collective-permute-start | bytes 811016 | tf_op jit(solution)/shard_map/ppermute | solution.py:109
  24.0 17.1 %copy-start.2 = (bf16[256,4096]{1,0:T(8,128)(2,1)S(1)}, bf16[256,4096]{1,0:T(8,128)(2,1)}, u32[]{:S(2)}) copy-start(bf16[256,4096]{1,0:T(8,128)(2,1)} %get-tuple-element.25) | copy-start | bytes 6291460
  24.0 28.7 %collective-permute-start.8 = (bf16[64,4096]{1,0:T(8,128)(2,1)}, bf16[64,4096]{1,0:T(8,128)(2,1)S(1)}, u32[]{:S(2)}, u32[]{:S(2)}) collective-permute-start(bf16[64,4096]{1,0:T(8,128)(2,1)} %get-tuple-element.24), channel_id=1, source_target_pairs={{0,16},{1,9},{2,18},{3,11},{4,20},{5,13},{6,22},{7,15},{8,24},{9,1... | collective-permute-start | bytes 1572872 | tf_op jit(solution)/shard_map/ppermute | solution.py:109
  25.6 15.1 %collective-permute-start.7 = (bf16[64,4096]{1,0:T(8,128)(2,1)}, bf16[64,4096]{1,0:T(8,128)(2,1)S(1)}, u32[]{:S(2)}, u32[]{:S(2)}) collective-permute-start(bf16[64,4096]{1,0:T(8,128)(2,1)} %get-tuple-element.24), channel_id=1, source_target_pairs={{0,8},{1,17},{2,10},{3,19},{4,12},{5,21},{6,14},{7,23},{8,0},{9,25... | collective-permute-start | bytes 1572872 | tf_op jit(solution)/shard_map/ppermute | solution.py:109
  28.5 23.7 %collective-permute-start.2 = (bf16[64,4224]{1,0:T(8,128)(2,1)S(1)}, bf16[64,4224]{1,0:T(8,128)(2,1)S(1)}, u32[]{:S(2)}, u32[]{:S(2)}) collective-permute-start(bf16[64,4224]{1,0:T(8,128)(2,1)S(1)} %pad_maximum_fusion.1), channel_id=1, source_target_pairs={{0,8},{1,17},{2,10},{3,19},{4,12},{5,21},{6,14},{7,23},{8,0},{9,25... | collective-permute-start | bytes 1622024 | tf_op jit(solution)/shard_map/ppermute | solution.py:109
  30.2 22.6 %collective-permute-start.3 = (bf16[64,4224]{1,0:T(8,128)(2,1)S(1)}, bf16[64,4224]{1,0:T(8,128)(2,1)S(1)}, u32[]{:S(2)}, u32[]{:S(2)}) collective-permute-start(bf16[64,4224]{1,0:T(8,128)(2,1)S(1)} %pad_maximum_fusion.1), channel_id=1, source_target_pairs={{0,16},{1,9},{2,18},{3,11},{4,20},{5,13},{6,22},{7,15},{8,24},{9,1... | collective-permute-start | bytes 1622024 | tf_op jit(solution)/shard_map/ppermute | solution.py:109
  40.6 15.0 %collective-permute-start.9 = (bf16[64,4096]{1,0:T(8,128)(2,1)S(1)}, bf16[64,4096]{1,0:T(8,128)(2,1)S(1)}, u32[]{:S(2)}, u32[]{:S(2)}) collective-permute-start(bf16[64,4096]{1,0:T(8,128)(2,1)S(1)} %collective-permute-done.7), channel_id=1, source_target_pairs={{0,16},{1,9},{2,18},{3,11},{4,20},{5,13},{6,22},{7,15},{8,24},{9,1... | collective-permute-start | bytes 1572872 | tf_op jit(solution)/shard_map/ppermute | solution.py:109
  52.2 9.4 %collective-permute-start.4 = (bf16[64,4224]{1,0:T(8,128)(2,1)S(1)}, bf16[64,4224]{1,0:T(8,128)(2,1)S(1)}, u32[]{:S(2)}, u32[]{:S(2)}) collective-permute-start(bf16[64,4224]{1,0:T(8,128)(2,1)S(1)} %collective-permute-done.2), channel_id=1, source_target_pairs={{0,16},{1,9},{2,18},{3,11},{4,20},{5,13},{6,22},{7,15},{8,24},{9,1... | collective-permute-start | bytes 1622024 | tf_op jit(solution)/shard_map/ppermute | solution.py:109
  55.7 11.0 %collective-permute-start.11 = (bf16[256,4096]{1,0:T(8,128)(2,1)S(1)}, bf16[256,4096]{1,0:T(8,128)(2,1)S(1)}, u32[]{:S(2)}, u32[]{:S(2)}) collective-permute-start(bf16[256,4096]{1,0:T(8,128)(2,1)S(1)} %constant_dynamic-update-slice_fusion.3), channel_id=1, source_target_pairs={{0,1},{1,0},{2,3},{3,2},{4,5},{5,4},{6,7},{7,6},{8,9},{9,8},{10,11... | collective-permute-start | bytes 6291464 | tf_op jit(solution)/shard_map/ppermute | solution.py:109
  61.6 4.6 %collective-permute-start.10 = (bf16[256,128]{1,0:T(8,128)(2,1)S(1)}, bf16[256,128]{1,0:T(8,128)(2,1)S(1)}, u32[]{:S(2)}, u32[]{:S(2)}) collective-permute-start(bf16[256,128]{1,0:T(8,128)(2,1)S(1)} %pad_maximum_fusion.5), channel_id=1, source_target_pairs={{0,1},{1,0},{2,3},{3,2},{4,5},{5,4},{6,7},{7,6},{8,9},{9,8},{10,11... | collective-permute-start | bytes 196616 | tf_op jit(solution)/shard_map/ppermute | solution.py:109
  61.9 6.1 %collective-permute-start.12 = (bf16[256,4096]{1,0:T(8,128)(2,1)S(1)}, bf16[256,4096]{1,0:T(8,128)(2,1)S(1)}, u32[]{:S(2)}, u32[]{:S(2)}) collective-permute-start(bf16[256,4096]{1,0:T(8,128)(2,1)S(1)} %pad_maximum_fusion), channel_id=1, source_target_pairs={{0,1},{1,0},{2,3},{3,2},{4,5},{5,4},{6,7},{7,6},{8,9},{9,8},{10,11... | collective-permute-start | bytes 6291464 | tf_op jit(solution)/shard_map/ppermute | solution.py:109
  62.8 1.9 %copy-start.1 = (bf16[2,192,4096]{2,1,0:T(8,128)(2,1)S(1)}, bf16[2,192,4096]{2,1,0:T(8,128)(2,1)}, u32[]{:S(2)}) copy-start(bf16[2,192,4096]{2,1,0:T(8,128)(2,1)} %param.12) | copy-start | bytes 9437188
  64.7 2.0 %copy-start.4 = (bf16[2,192,4096]{2,1,0:T(8,128)(2,1)S(1)}, bf16[2,192,4096]{2,1,0:T(8,128)(2,1)}, u32[]{:S(2)}) copy-start(bf16[2,192,4096]{2,1,0:T(8,128)(2,1)} %param.13) | copy-start | bytes 9437188
  75.0 8.8 %collective-permute-start.13 = (bf16[256,4096]{1,0:T(8,128)(2,1)S(1)}, bf16[256,4096]{1,0:T(8,128)(2,1)S(1)}, u32[]{:S(2)}, u32[]{:S(2)}) collective-permute-start(bf16[256,4096]{1,0:T(8,128)(2,1)S(1)} %fusion.2), channel_id=1, source_target_pairs={{0,1},{1,0},{2,3},{3,2},{4,5},{5,4},{6,7},{7,6},{8,9},{9,8},{10,11... | collective-permute-start | bytes 6291464 | tf_op jit(solution)/shard_map/ppermute | solution.py:109
  75.1 7.3 %collective-permute-start.19 = (f32[2,256]{1,0:T(2,128)S(1)}, f32[2,256]{1,0:T(2,128)S(1)}, u32[]{:S(2)}, u32[]{:S(2)}) collective-permute-start(f32[2,256]{1,0:T(2,128)S(1)} %pad_maximum_fusion.6), channel_id=1, source_target_pairs={{0,1},{1,0},{2,3},{3,2},{4,5},{5,4},{6,7},{7,6},{8,9},{9,8},{10,11... | collective-permute-start | bytes 6152 | tf_op jit(solution)/shard_map/ppermute | solution.py:109
  82.4 6.5 %collective-permute-start.20 = (f32[2,128]{1,0:T(2,128)S(1)}, f32[2,128]{1,0:T(2,128)S(1)}, u32[]{:S(2)}, u32[]{:S(2)}) collective-permute-start(f32[2,128]{1,0:T(2,128)S(1)} %split.73), channel_id=1, source_target_pairs={{0,16},{1,9},{2,18},{3,11},{4,20},{5,13},{6,22},{7,15},{8,24},{9,1... | collective-permute-start | bytes 3080 | tf_op jit(solution)/shard_map/ppermute | solution.py:109
  85.4 14.9 %collective-permute-start.14 = (bf16[128,4096]{1,0:T(8,128)(2,1)S(1)}, bf16[128,4096]{1,0:T(8,128)(2,1)S(1)}, u32[]{:S(2)}, u32[]{:S(2)}) collective-permute-start(bf16[128,4096]{1,0:T(8,128)(2,1)S(1)} %split.65), channel_id=1, source_target_pairs={{0,16},{1,9},{2,18},{3,11},{4,20},{5,13},{6,22},{7,15},{8,24},{9,1... | collective-permute-start | bytes 3145736 | tf_op jit(solution)/shard_map/ppermute | solution.py:109
  89.0 3.6 %collective-permute-start.21 = (f32[2,64]{1,0:T(2,128)S(1)}, f32[2,64]{1,0:T(2,128)S(1)}, u32[]{:S(2)}, u32[]{:S(2)}) collective-permute-start(f32[2,64]{1,0:T(2,128)S(1)} %split.59), channel_id=1, source_target_pairs={{0,8},{1,17},{2,10},{3,19},{4,12},{5,21},{6,14},{7,23},{8,0},{9,25... | collective-permute-start | bytes 1544 | tf_op jit(solution)/shard_map/ppermute | solution.py:109
  92.8 11.1 %collective-permute-start.22 = (f32[2,32]{1,0:T(2,128)S(1)}, f32[2,32]{1,0:T(2,128)S(1)}, u32[]{:S(2)}, u32[]{:S(2)}) collective-permute-start(f32[2,32]{1,0:T(2,128)S(1)} %split.61), channel_id=1, source_target_pairs={{0,2},{1,3},{2,0},{3,1},{4,6},{5,7},{6,4},{7,5},{8,10},{9,11},{10,... | collective-permute-start | bytes 776 | tf_op jit(solution)/shard_map/ppermute | solution.py:109
  100.5 9.2 %collective-permute-start.15 = (bf16[64,4096]{1,0:T(8,128)(2,1)S(1)}, bf16[64,4096]{1,0:T(8,128)(2,1)S(1)}, u32[]{:S(2)}, u32[]{:S(2)}) collective-permute-start(bf16[64,4096]{1,0:T(8,128)(2,1)S(1)} %split.67), channel_id=1, source_target_pairs={{0,8},{1,17},{2,10},{3,19},{4,12},{5,21},{6,14},{7,23},{8,0},{9,25... | collective-permute-start | bytes 1572872 | tf_op jit(solution)/shard_map/ppermute | solution.py:109
  104.0 10.5 %collective-permute-start.23 = (f32[2,16]{1,0:T(2,128)S(1)}, f32[2,16]{1,0:T(2,128)S(1)}, u32[]{:S(2)}, u32[]{:S(2)}) collective-permute-start(f32[2,16]{1,0:T(2,128)S(1)} %split.63), channel_id=1, source_target_pairs={{0,4},{1,5},{2,6},{3,7},{4,0},{5,1},{6,2},{7,3},{8,12},{9,13},{10,... | collective-permute-start | bytes 392 | tf_op jit(solution)/shard_map/ppermute | solution.py:109
  109.9 12.2 %collective-permute-start.16 = (bf16[16,4096]{1,0:T(8,128)(2,1)S(1)}, bf16[16,4096]{1,0:T(8,128)(2,1)S(1)}, u32[]{:S(2)}, u32[]{:S(2)}) collective-permute-start(bf16[16,4096]{1,0:T(8,128)(2,1)S(1)} %get-tuple-element.21), channel_id=1, source_target_pairs={{0,4},{1,5},{2,6},{3,7},{4,0},{5,1},{6,2},{7,3},{8,12},{9,13},{10,... | collective-permute-start | bytes 393224 | tf_op jit(solution)/shard_map/ppermute | solution.py:109
  112.8 9.4 %collective-permute-start.18 = (bf16[16,4096]{1,0:T(8,128)(2,1)S(1)}, bf16[16,4096]{1,0:T(8,128)(2,1)S(1)}, u32[]{:S(2)}, u32[]{:S(2)}) collective-permute-start(bf16[16,4096]{1,0:T(8,128)(2,1)S(1)} %get-tuple-element.22), channel_id=1, source_target_pairs={{0,6},{1,7},{2,4},{3,5},{4,2},{5,3},{6,0},{7,1},{8,14},{9,15},{10,... | collective-permute-start | bytes 393224 | tf_op jit(solution)/shard_map/ppermute | solution.py:109
  114.0 8.3 %collective-permute-start.17 = (bf16[16,4096]{1,0:T(8,128)(2,1)S(1)}, bf16[16,4096]{1,0:T(8,128)(2,1)S(1)}, u32[]{:S(2)}, u32[]{:S(2)}) collective-permute-start(bf16[16,4096]{1,0:T(8,128)(2,1)S(1)} %get-tuple-element.23), channel_id=1, source_target_pairs={{0,2},{1,3},{2,0},{3,1},{4,6},{5,7},{6,4},{7,5},{8,10},{9,11},{10,... | collective-permute-start | bytes 393224 | tf_op jit(solution)/shard_map/ppermute | solution.py:109
